TPU v7x, 512 devices: a whole 4x8x8 slice. The times are simulated.
512 devices in a mesh: grp: 256 (over z, y, x), mem: 2 (over core).
Axes of the slice: x: 4, y: 8, z: 8, core: 2. Of those that a mesh axis runs over, the one named last changes fastest.
Arguments:
- state: float32 [5, 125, 131072], P(None, None, ('grp', 'mem')), may hold values from -6 to 6
- rhs: float32 [5, 125, 131072], P(None, None, ('grp', 'mem')), may hold values from -6 to 6
- fine_diag: float32 [5, 125, 131072], P(None, None, ('grp', 'mem')), may hold values from 2 to 20
- q_fine: float32 [125, 125], replicated, may hold values from -0.5 to 0.5
- var_mix: float32 [5, 5], replicated, may hold values from -2.5 to 2.5
- mem_count: int32 [512, 2], P(('grp', 'mem')), may hold values from 42 to 128, as said below
- grp_count: int32 [512, 2], P(('grp', 'mem')), may hold values from 85 to 256, as said below
- send_mem_idx: int32 [512, 2, 128], P(('grp', 'mem')), may hold values from 0 to 1535
- send_grp_idx: int32 [512, 2, 256], P(('grp', 'mem')), may hold values from 0 to 1535
- face_src: int32 [6, 131072], P(None, ('grp', 'mem')), may hold values from 0 to 2304
- coarse_diag: float32 [5, 8, 131072], P(None, None, ('grp', 'mem')), may hold values from 3 to 12
- q_coarse: float32 [8, 8], replicated, may hold values from -2 to 2
- g_coarse: float32 [6, 8, 8], replicated, may hold values from -0.875 to 0.875
- owner: int32 [131072, 1], P(('grp', 'mem')), may hold values from 0 to 1; in each aligned block of 256 rows (0 to 255, 256 to 511, ...) at most 128 rows name the same one
- coarse_nbr: int32 [6, 131072], P(None, ('grp', 'mem')), may hold values from 0 to 768
Outputs:
- residual: float32 [5, 125, 131072], P(None, None, ('grp', 'mem'))
- correction: float32 [5, 125, 131072], P(None, None, ('grp', 'mem'))
Inputs may be any that keep to these rules, and one draw needn't show every extreme that they name: `mem_count`: entries for a partition's own member are not used; some entry equals 128. `grp_count`: some entry equals 256. At most 128 elements of one partition have one owner, and exactly 128 in some partition.
All inputs are finite; a program needn't handle non-finite values.
Results may differ from a plain program's by a relative error of at most 0.0003.
Values sent between devices are 32-bit elements; how exact they have to be, the bound alone decides.
A program may use at most 64 MiB of HBM per device.

v0:
```python
import jax
import jax.numpy as jnp
from jax import lax
from jax.sharding import PartitionSpec as P

OMEGA = 0.8
HIGH = lax.Precision.HIGHEST


def padded_2(block, sides, width):
    for axis, dim in sides:
        count = lax.axis_size(axis)
        forward = [(i, i + 1) for i in range(count - 1)]
        backward = [(target, source) for source, target in forward]
        low = lax.ppermute(
            lax.slice_in_dim(block, block.shape[dim] - width, None, axis=dim), axis, forward
        )
        high = lax.ppermute(lax.slice_in_dim(block, 0, width, axis=dim), axis, backward)
        block = jnp.concatenate([low, block, high], axis=dim)
    return block


def mult(form, left, right):
    return jnp.einsum(form, left, right, precision=HIGH)


def fine_tables():
    points = jnp.arange(125, dtype=jnp.int32)
    coords = [points // 25, points // 5 % 5, points % 5]
    blocks = []
    for face in range(6):
        along = face // 2
        others = [c for b, c in enumerate(coords) if b != along]
        index = others[0] * 5 + others[1]
        on_face = coords[along] == 4 * (face % 2)
        blocks.append(
            (
                (index[None, :] == jnp.arange(25, dtype=jnp.int32)[:, None]) & on_face[None, :]
            ).astype(jnp.float32)
        )
    extract = jnp.concatenate(blocks, axis=0)
    lift = extract.T
    nodes = -1.0 + 0.5 * jnp.arange(5, dtype=jnp.float32)
    basis = jnp.stack([(1.0 - nodes) / 2.0, (1.0 + nodes) / 2.0], axis=1)
    prolong = jnp.einsum("ia,jb,kc->ijkabc", basis, basis, basis).reshape(125, 8)
    restrict = prolong.T * 0.064
    return (extract, lift, prolong, restrict)


def trace_cols(field, extract):
    nvar, npts, elems = field.shape
    faces = mult("fp,vpe->vfe", extract, field)
    return faces.reshape(nvar, 6, 25, elems).transpose(0, 2, 1, 3).reshape(nvar * 25, 6 * elems)


def build_sends(faces, mcount, gcount, midx, gidx, member):
    members, mslots = midx.shape
    gslots = gidx.shape[1]
    rows = faces.shape[0]
    mkeep = (
        (jnp.arange(mslots, dtype=jnp.int32)[None, :] < mcount[:, None])
        & (jnp.arange(members, dtype=jnp.int32)[:, None] != member)
    ).astype(jnp.float32)
    gkeep = (jnp.arange(gslots, dtype=jnp.int32)[None, :] < gcount[:, None]).astype(jnp.float32)
    to_members = (
        jnp.take(faces, midx.reshape(-1), axis=1).reshape(rows, members, mslots).transpose(1, 0, 2)
        * mkeep[:, None, :]
    )
    to_groups = (
        jnp.take(faces, gidx.reshape(-1), axis=1).reshape(rows, 2, gslots).transpose(1, 0, 2)
        * gkeep[:, None, :]
    )
    return (to_members, to_groups)


def local_residual(
    field, rhs, diag, q_fine, var_mix, faces, from_members, from_prev, from_next, source, lift
):
    nvar, npts, elems = field.shape
    rows = faces.shape[0]
    columns = jnp.concatenate(
        [
            faces,
            from_members.transpose(1, 0, 2).reshape(rows, -1),
            from_prev,
            from_next,
            jnp.zeros((rows, 1), jnp.float32),
        ],
        axis=1,
    )
    near = (
        jnp.take(columns, source.reshape(-1), axis=1)
        .reshape(nvar, 25, 6, elems)
        .transpose(0, 2, 1, 3)
        .reshape(nvar, 150, elems)
    )
    applied = (
        diag * field
        + mult("pq,vqe->vpe", q_fine, field)
        + mult("vw,wpe->vpe", var_mix, field)
        - mult("pf,vfe->vpe", lift, near)
    )
    return rhs - applied


def ranks(own, members):
    onehot = (own[None, :] == jnp.arange(members, dtype=jnp.int32)[:, None]).astype(jnp.int32)
    return jnp.sum((jnp.cumsum(onehot, axis=1) - 1) * onehot, axis=0)


def second_sweep(first, slot_rhs, slot_diag, rim, nbr_idx, q_coarse, g_coarse):
    width = first.shape[1]
    nvar = first.shape[0] // 8
    columns = jnp.concatenate([rim, jnp.zeros((rim.shape[0], 1), jnp.float32)], axis=1)
    near = jnp.take(columns, nbr_idx.reshape(-1), axis=1).reshape(nvar, 8, 6, width)
    inner = mult("ab,vbs->vas", q_coarse, first.reshape(nvar, 8, width))
    across = mult("fab,vbfs->vas", g_coarse, near)
    applied = slot_diag * first + (inner - across).reshape(nvar * 8, width)
    return first + OMEGA * (slot_rhs - applied) / slot_diag


def shards(
    state,
    rhs,
    fine_diag,
    q_fine,
    var_mix,
    mem_count,
    grp_count,
    send_mem_idx,
    send_grp_idx,
    face_src,
    coarse_diag,
    q_coarse,
    g_coarse,
    owner,
    coarse_nbr,
):
    extract, lift, prolong, restrict = fine_tables()
    nvar, npts, elems = state.shape
    members = lax.axis_size("mem")
    member = lax.axis_index("mem")
    faces = trace_cols(state, extract)
    to_members, to_groups = build_sends(
        faces, mem_count[0], grp_count[0], send_mem_idx[0], send_grp_idx[0], member
    )
    from_members = lax.all_to_all(to_members, "mem", split_axis=0, concat_axis=0, tiled=True)
    padded = padded_2(to_groups, (("grp", 0),), 1)
    resid = local_residual(
        state,
        rhs,
        fine_diag,
        q_fine,
        var_mix,
        faces,
        from_members,
        padded[0],
        padded[3],
        face_src,
        lift,
    )
    restricted = mult("cp,vpe->vce", restrict, resid).reshape(nvar * 8, elems)
    cdiag = coarse_diag.reshape(nvar * 8, elems)
    own = owner[:, 0]
    slot_rank = ranks(own, members)
    scap = elems // 2
    capc = members * scap
    target = own * scap + slot_rank
    select = (target[:, None] == jnp.arange(capc, dtype=jnp.int32)[None, :]).astype(jnp.float32)
    occupied = jnp.sum(select, axis=0)
    blocks_rhs = jnp.dot(restricted, select, precision=HIGH).reshape(nvar * 8, members, scap)
    blocks_diag = (jnp.dot(cdiag, select, precision=HIGH) + (1.0 - occupied)[None, :]).reshape(
        nvar * 8, members, scap
    )
    got_rhs, got_diag = (
        lax.all_to_all(blocks_rhs, "mem", split_axis=1, concat_axis=1, tiled=True),
        lax.all_to_all(blocks_diag, "mem", split_axis=1, concat_axis=1, tiled=True),
    )
    slot_rhs = got_rhs.reshape(nvar * 8, capc)
    slot_diag = got_diag.reshape(nvar * 8, capc)
    first = OMEGA * slot_rhs / slot_diag
    rim = padded_2(first, (("grp", 1),), capc)
    second = second_sweep(first, slot_rhs, slot_diag, rim, coarse_nbr, q_coarse, g_coarse)
    returned = lax.all_to_all(
        second.reshape(nvar * 8, members, scap), "mem", split_axis=1, concat_axis=1, tiled=True
    ).reshape(nvar * 8, capc)
    picked = jnp.dot(returned, select.T, precision=HIGH)
    correction = mult("pc,vce->vpe", prolong, picked.reshape(nvar, 8, elems))
    return (resid, correction)


def solution(mesh):
    return jax.shard_map(
        shards,
        mesh=mesh,
        in_specs=(
            P(None, None, ("grp", "mem")),
            P(None, None, ("grp", "mem")),
            P(None, None, ("grp", "mem")),
            P(),
            P(),
            P(("grp", "mem"), None),
            P(("grp", "mem"), None),
            P(("grp", "mem"), None, None),
            P(("grp", "mem"), None, None),
            P(None, ("grp", "mem")),
            P(None, None, ("grp", "mem")),
            P(),
            P(),
            P(("grp", "mem"), None),
            P(None, ("grp", "mem")),
        ),
        out_specs=(P(None, None, ("grp", "mem")), P(None, None, ("grp", "mem"))),
        check_vma=False,
    )
```

profile of v0, /device:TPU:255, one launch (start us, length us, event | category | flops | bytes accessed | tf_op | source)
XLA Modules:
  0.0 79.1 jit_solution(12510788946154247574)
XLA Ops:
  0.8 0.7 concatenate.12
  1.6 1.6 %convolution_bitcast_fusion = f32[5,150,256]{2,1,0:T(8,128)S(1)} fusion(f32[5,125,256]{2,1,0:T(8,128)} %param.15, pred[150,125]{1,0:T(8,128)(4,1)S(1)} %concatenate.12), kind=kOutput, calls=%fused_computation.4 | convolution fusion | flops 288000000 | bytes 1426750 | tf_op jit(solution)/shard_map/fp,vpe->vfe/dot_general | solution.py:24
  3.2 0.1 reshape.411
  3.3 0.5 copy.81
  3.8 0.3 copy.103
  4.1 0.3 copy.84
  4.4 0.4 copy-done.12
  4.8 0.7 gather_fusion
  5.6 0.1 and_convert_fusion
  5.6 0.8 multiply_bitcast_fusion.2
  6.4 4.0 %all-to-all-start = ((f32[2,125,128]{1,2,0:T(8,128)}), f32[2,125,128]{1,2,0:T(8,128)S(1)}, u32[]{:S(2)}, u32[]{:S(2)}) async-start(f32[2,125,128]{1,2,0:T(8,128)} %multiply_bitcast_fusion.2), calls=%async_computation | async-start | bytes 262144 | tf_op jit(solution)/shard_map/all_to_all | solution.py:147
  10.5 1.0 %gather_fusion.1 = f32[512,125]{1,0:T(8,128)S(1)} fusion(f32[125,1536]{0,1:T(8,128)S(1)} %copy.84, s32[1024]{0:T(1024)S(1)} %get-tuple-element.26), kind=kCustom, calls=%fused_computation.1 | custom fusion | bytes 514048 | tf_op jit(solution)/shard_map/jit(_take)/gather | solution.py:70
  11.6 0.2 multiply_bitcast_fusion
  11.8 0.7 fusion.47
  12.5 4.3 %collective-permute-start = (f32[1,125,256]{1,2,0:T(8,128)}, f32[1,125,256]{1,2,0:T(8,128)}, u32[]{:S(2)}, u32[]{:S(2)}) collective-permute-start(f32[1,125,256]{1,2,0:T(8,128)} %get-tuple-element.11), channel_id=1, source_target_pairs={{0,2},{2,4},{4,6},{6,8},{8,10},{10,12},{12,14},{14,16},{16,18},{18... | collective-permute-start | bytes 384008 | tf_op jit(solution)/shard_map/ppermute | solution.py:15
  16.9 1.9 %collective-permute-start.1 = (f32[1,125,256]{1,2,0:T(8,128)}, f32[1,125,256]{1,2,0:T(8,128)S(1)}, u32[]{:S(2)}, u32[]{:S(2)}) collective-permute-start(f32[1,125,256]{1,2,0:T(8,128)} %get-tuple-element.10), channel_id=1, source_target_pairs={{2,0},{4,2},{6,4},{8,6},{10,8},{12,10},{14,12},{16,14},{18,16},{20... | collective-permute-start | bytes 384008 | tf_op jit(solution)/shard_map/ppermute | solution.py:18
  18.9 0.6 compare_and_fusion.1
  19.5 0.6 pad_clamp_fusion.1
  20.2 1.3 %fusion.6 = f32[5,125,256]{2,0,1:T(8,128)S(1)} fusion(f32[5,125,256]{2,1,0:T(8,128)S(1)} %copy-done.1, f32[5,5]{1,0:T(8,128)S(1)} %copy-done.13), kind=kOutput, calls=%fused_computation.18 | convolution fusion | flops 9600000 | bytes 1280100 | tf_op jit(solution)/shard_map/vw,wpe->vpe/dot_general | solution.py:24
  21.6 0.1 multiply_bitcast_fusion.1
  21.7 0.6 reduce-window.6
  22.3 0.2 slice_reduce_fusion
  22.5 0.2 reduce-window.9
  22.7 0.1 select_reduce_fusion
  22.8 0.1 convert_reduce_fusion
  22.9 0.6 compare_and_fusion
  23.6 0.3 fusion.5
  23.9 0.6 multiply_add_fusion
  24.5 1.1 %copy.77 = f32[5,125,256]{1,2,0:T(8,128)} copy(f32[5,125,256]{2,1,0:T(8,128)S(1)} %copy-done.1) | data formatting | bytes 1280000 | tf_op args[0]
  25.6 1.2 %copy.80 = f32[5,125,256]{1,2,0:T(8,128)} copy(f32[5,125,256]{2,0,1:T(8,128)S(1)} %fusion.6) | data formatting | bytes 1280000 | tf_op jit(solution)/shard_map/vw,wpe->vpe/dot_general | solution.py:24
  26.8 2.3 %copy.76 = f32[5,125,256]{1,2,0:T(8,128)} copy(f32[5,125,256]{2,1,0:T(8,128)} %param.17) | data formatting | bytes 1280000 | tf_op args[2]
  29.0 1.1 %copy.87 = f32[5,125,256]{1,2,0:T(8,128)} copy(f32[5,125,256]{2,1,0:T(8,128)S(1)} %copy-done.5) | data formatting | bytes 1280000 | tf_op args[1]
  30.1 0.1 reshape.416
  30.2 0.6 copy.121
  30.8 3.6 %all-to-all-start.2 = ((f32[40,2,128]{2,0,1:T(8,128)}), f32[40,2,128]{2,0,1:T(8,128)S(1)}, u32[]{:S(2)}, u32[]{:S(2)}) async-start(f32[40,2,128]{2,0,1:T(8,128)} %bitcast.129), calls=%async_computation.2 | async-start | bytes 81920 | tf_op jit(solution)/shard_map/all_to_all | solution.py:177
  34.4 0.9 %bitcast_dynamic-update-slice_fusion.1 = f32[125,2305]{0,1:T(8,128)S(1)} fusion(f32[125,2305]{0,1:T(8,128)S(1)} %constant_dynamic-update-slice_fusion, f32[1,125,256]{1,2,0:T(8,128)} %collective-permute-done), kind=kLoop, calls=%fused_computation.32 | loop fusion | bytes 259072
  35.4 3.0 %gather_fusion.2 = f32[1536,125]{1,0:T(8,128)S(1)} fusion(f32[125,2305]{0,1:T(8,128)S(1)} %dynamic-update-slice.4, s32[2048]{0:T(1024)} %pad_clamp_fusion.1), kind=kCustom, calls=%fused_computation.2 | custom fusion | bytes 1542144 | tf_op jit(solution)/shard_map/jit(_take)/gather | solution.py:92
  38.4 0.3 copy.85
  38.8 0.2 gather.29
  39.0 0.5 copy-done.11
  39.4 0.1 select_bitcast_fusion
  39.5 0.3 copy.86
  39.8 0.1 reshape.415
  40.0 1.2 %convolution_bitcast_fusion.1 = f32[5,125,256]{1,2,0:T(8,128)S(1)} fusion(f32[5,150,256]{2,1,0:T(8,128)S(1)} %reshape.415, pred[150,125]{1,0:T(8,128)(4,1)S(1)} %concatenate.12), kind=kOutput, calls=%fused_computation.5 | convolution fusion | flops 288000000 | bytes 1426750 | tf_op jit(solution)/shard_map/pf,vfe->vpe/dot_general | solution.py:24
  41.2 0.1 copy-done.4
  41.3 2.4 %fusion.3 = f32[5,125,256]{1,2,0:T(8,128)S(1)} fusion(f32[5,125,256]{1,2,0:T(8,128)} %copy.87, f32[5,125,256]{1,2,0:T(8,128)S(1)} %convolution_bitcast_fusion.1, f32[5,125,256]{1,2,0:T(8,128)S(1)} %copy-done.2, f32[5,125,256]{2,1,0:T(8,128)S(1)} %copy-done.1, f32[5,125,256]{1,2,0:T(8,128)S(1)} %copy-done.4, f32[5,125,256]{1,2,0:T(8,128)S(1)} %copy-done.3, ...), kind=kOutput, calls=%fused_computation.10 | convolution fusion | flops 240800000 | bytes 4542500 | tf_op jit(solution)/shard_map/pq,vqe->vpe/dot_general | solution.py:24
  43.7 0.7 convolution_bitcast_fusion.5
  44.4 0.4 fusion.11
  44.7 3.4 %all_to_all.20 = f32[40,2,128]{2,0,1:T(8,128)S(1)} all-to-all(f32[40,2,128]{2,0,1:T(8,128)S(1)} %fusion.11), channel_id=1, replica_groups=mesh['grp'=256,'mem'=2] {'mem'}, dimensions={1} | all-to-all | bytes 81920 | tf_op jit(solution)/shard_map/all_to_all | solution.py:176
  48.2 9.1 %collective-permute-start.2 = (f32[40,256]{1,0:T(8,128)S(1)}, f32[40,256]{1,0:T(8,128)S(1)}, u32[]{:S(2)}, u32[]{:S(2)}) collective-permute-start(f32[40,256]{1,0:T(8,128)S(1)} %bitcast.140), channel_id=1, source_target_pairs={{0,2},{2,4},{4,6},{6,8},{8,10},{10,12},{12,14},{14,16},{16,18},{18... | collective-permute-start | bytes 122888 | tf_op jit(solution)/shard_map/ppermute | solution.py:15
  57.3 2.1 %collective-permute-start.3 = (f32[40,256]{1,0:T(8,128)S(1)}, f32[40,256]{1,0:T(8,128)S(1)}, u32[]{:S(2)}, u32[]{:S(2)}) collective-permute-start(f32[40,256]{1,0:T(8,128)S(1)} %bitcast.141), channel_id=1, source_target_pairs={{2,0},{4,2},{6,4},{8,6},{10,8},{12,10},{14,12},{16,14},{18,16},{20... | collective-permute-start | bytes 122888 | tf_op jit(solution)/shard_map/ppermute | solution.py:18
  59.4 0.1 reshape.464
  59.5 1.1 %copy.96 = f32[5,125,256]{2,1,0:T(8,128)} copy(f32[5,125,256]{1,2,0:T(8,128)S(1)} %fusion.3) | data formatting | bytes 1280000
  60.7 6.8 %collective-permute-done.3 = f32[40,256]{1,0:T(8,128)S(1)} collective-permute-done((f32[40,256]{1,0:T(8,128)S(1)}, f32[40,256]{1,0:T(8,128)S(1)}, u32[]{:S(2)}, u32[]{:S(2)}) %collective-permute-start.3) | collective-permute-done | bytes 40992 | tf_op jit(solution)/shard_map/ppermute | solution.py:18
  67.5 0.2 copy.92
  67.7 2.6 %gather_fusion.3 = f32[1536,40]{1,0:T(8,128)S(1)} fusion(f32[40,769]{0,1:T(8,128)S(1)} %copy.92, s32[2048]{0:T(1024)S(1)} %pad_clamp_fusion), kind=kCustom, calls=%fused_computation.3 | custom fusion | bytes 497664 | tf_op jit(solution)/shard_map/jit(_take)/gather | solution.py:115
  70.3 0.2 copy.93
  70.5 0.3 convolution_bitcast_fusion.4
  70.8 0.1 copy-done.14
  71.0 0.2 fusion.4
  71.2 5.2 %all_to_all.21 = f32[40,2,128]{2,0,1:T(8,128)S(1)} all-to-all(f32[40,2,128]{2,0,1:T(8,128)S(1)} %fusion.27), channel_id=1, replica_groups=mesh['grp'=256,'mem'=2] {'mem'}, dimensions={1} | all-to-all | bytes 81920 | tf_op jit(solution)/shard_map/all_to_all | solution.py:184
  76.4 0.3 fusion.9
  76.8 1.2 %convolution_bitcast_fusion.3 = f32[5,125,256]{1,2,0:T(8,128)S(1)} fusion(f32[5,8,256]{2,1,0:T(8,128)S(1)} %fusion.9, f32[125,8,1]{0,1,2:T(8,128)S(1)} %reshape.464), kind=kOutput, calls=%fused_computation.11 | convolution fusion | flops 15360000 | bytes 684960 | tf_op jit(solution)/shard_map/pc,vce->vpe/dot_general | solution.py:24
  78.0 1.1 %copy.97 = f32[5,125,256]{2,1,0:T(8,128)} copy(f32[5,125,256]{1,2,0:T(8,128)S(1)} %convolution_bitcast_fusion.3) | data formatting | bytes 1280000
  (87 shorter events, 0.9 us)
Async XLA Ops:
  0.6 40.6 %copy-start = (f32[125,125]{1,0:T(8,128)S(1)}, f32[125,125]{1,0:T(8,128)}, u32[]{:S(2)}) copy-start(f32[125,125]{1,0:T(8,128)} %param.18) | copy-start | bytes 187504
  4.1 0.7 copy-start.12
  4.1 0.7 copy-start.15
  4.1 1.5 %copy-start.18 = (s32[1,2]{1,0:T(1,128)S(1)}, s32[1,2]{1,0:T(1,128)}, u32[]{:S(2)}) copy-start(s32[1,2]{1,0:T(1,128)} %param.20) | copy-start | bytes 28
  6.4 24.4 %all-to-all-start = ((f32[2,125,128]{1,2,0:T(8,128)}), f32[2,125,128]{1,2,0:T(8,128)S(1)}, u32[]{:S(2)}, u32[]{:S(2)}) async-start(f32[2,125,128]{1,2,0:T(8,128)} %multiply_bitcast_fusion.2), calls=%async_computation | async-start | bytes 262144 | tf_op jit(solution)/shard_map/all_to_all | solution.py:147
  10.5 1.0 %copy-start.19 = (s32[1,2]{1,0:T(1,128)S(1)}, s32[1,2]{1,0:T(1,128)}, u32[]{:S(2)}) copy-start(s32[1,2]{1,0:T(1,128)} %param.21) | copy-start | bytes 28
  11.6 7.3 %copy-start.6 = (s32[6,256]{1,0:T(8,128)S(1)}, s32[6,256]{1,0:T(8,128)}, u32[]{:S(2)}) copy-start(s32[6,256]{1,0:T(8,128)} %param.24) | copy-start | bytes 18436
  11.8 8.4 %copy-start.1 = (f32[5,125,256]{2,1,0:T(8,128)S(1)}, f32[5,125,256]{2,1,0:T(8,128)}, u32[]{:S(2)}) copy-start(f32[5,125,256]{2,1,0:T(8,128)} %param.15) | copy-start | bytes 1920004
  11.8 8.4 %copy-start.13 = (f32[5,5]{1,0:T(8,128)S(1)}, f32[5,5]{1,0:T(8,128)}, u32[]{:S(2)}) copy-start(f32[5,5]{1,0:T(8,128)} %param.19) | copy-start | bytes 304
  12.5 21.9 %collective-permute-start = (f32[1,125,256]{1,2,0:T(8,128)}, f32[1,125,256]{1,2,0:T(8,128)}, u32[]{:S(2)}, u32[]{:S(2)}) collective-permute-start(f32[1,125,256]{1,2,0:T(8,128)} %get-tuple-element.11), channel_id=1, source_target_pairs={{0,2},{2,4},{4,6},{6,8},{8,10},{10,12},{12,14},{14,16},{16,18},{18... | collective-permute-start | bytes 384008 | tf_op jit(solution)/shard_map/ppermute | solution.py:15
  16.9 18.5 %collective-permute-start.1 = (f32[1,125,256]{1,2,0:T(8,128)}, f32[1,125,256]{1,2,0:T(8,128)S(1)}, u32[]{:S(2)}, u32[]{:S(2)}) collective-permute-start(f32[1,125,256]{1,2,0:T(8,128)} %get-tuple-element.10), channel_id=1, source_target_pairs={{2,0},{4,2},{6,4},{8,6},{10,8},{12,10},{14,12},{16,14},{18,16},{20... | collective-permute-start | bytes 384008 | tf_op jit(solution)/shard_map/ppermute | solution.py:18
  18.9 2.8 %copy-start.9 = (s32[256,1]{0,1:T(1,128)S(1)}, s32[256,1]{0,1:T(1,128)}, u32[]{:S(2)}) copy-start(s32[256,1]{0,1:T(1,128)} %param.28) | copy-start | bytes 3076
  18.9 4.1 %copy-start.7 = (s32[6,256]{1,0:T(8,128)S(1)}, s32[6,256]{1,0:T(8,128)}, u32[]{:S(2)}) copy-start(s32[6,256]{1,0:T(8,128)} %param.29) | copy-start | bytes 18436
  19.5 4.1 %copy-start.20 = (f32[5,8,256]{2,1,0:T(8,128)S(1)}, f32[5,8,256]{2,1,0:T(8,128)}, u32[]{:S(2)}) copy-start(f32[5,8,256]{2,1,0:T(8,128)} %param.25) | copy-start | bytes 122884
  22.8 4.0 %copy-start.16 = (s32[256,1]{0,1:T(1,128)}, s32[256,1]{0,1:T(1,128)S(1)}, u32[]{:S(2)}) copy-start(s32[256,1]{0,1:T(1,128)S(1)} %multiply_add_fusion.1) | copy-start | bytes 3076
  26.8 2.3 %copy-start.5 = (f32[5,125,256]{2,1,0:T(8,128)S(1)}, f32[5,125,256]{2,1,0:T(8,128)}, u32[]{:S(2)}) copy-start(f32[5,125,256]{2,1,0:T(8,128)} %param.16) | copy-start | bytes 1920004
  30.8 13.9 %all-to-all-start.2 = ((f32[40,2,128]{2,0,1:T(8,128)}), f32[40,2,128]{2,0,1:T(8,128)S(1)}, u32[]{:S(2)}, u32[]{:S(2)}) async-start(f32[40,2,128]{2,0,1:T(8,128)} %bitcast.129), calls=%async_computation.2 | async-start | bytes 81920 | tf_op jit(solution)/shard_map/all_to_all | solution.py:177
  38.7 0.7 copy-start.11
  39.8 1.4 %copy-start.2 = (f32[5,125,256]{1,2,0:T(8,128)S(1)}, f32[5,125,256]{1,2,0:T(8,128)}, u32[]{:S(2)}) copy-start(f32[5,125,256]{1,2,0:T(8,128)} %copy.80) | copy-start | bytes 1920004
  39.9 1.3 %copy-start.3 = (f32[5,125,256]{1,2,0:T(8,128)S(1)}, f32[5,125,256]{1,2,0:T(8,128)}, u32[]{:S(2)}) copy-start(f32[5,125,256]{1,2,0:T(8,128)} %copy.77) | copy-start | bytes 1920004
  40.0 1.4 %copy-start.4 = (f32[5,125,256]{1,2,0:T(8,128)S(1)}, f32[5,125,256]{1,2,0:T(8,128)}, u32[]{:S(2)}) copy-start(f32[5,125,256]{1,2,0:T(8,128)} %copy.76) | copy-start | bytes 1920004
  41.3 3.0 %copy-start.17 = (s32[256,1]{0,1:T(1,128)S(1)}, s32[256,1]{0,1:T(1,128)}, u32[]{:S(2)}) copy-start(s32[256,1]{0,1:T(1,128)} %copy-done.16) | copy-start | bytes 3076
  41.3 3.0 %copy-start.21 = (s32[2,128]{1,0:T(2,128)S(1)}, s32[2,128]{1,0:T(2,128)}, u32[]{:S(2)}) copy-start(s32[2,128]{1,0:T(2,128)} %multiply_add_fusion) | copy-start | bytes 3076
  48.2 12.5 %collective-permute-start.2 = (f32[40,256]{1,0:T(8,128)S(1)}, f32[40,256]{1,0:T(8,128)S(1)}, u32[]{:S(2)}, u32[]{:S(2)}) collective-permute-start(f32[40,256]{1,0:T(8,128)S(1)} %bitcast.140), channel_id=1, source_target_pairs={{0,2},{2,4},{4,6},{6,8},{8,10},{10,12},{12,14},{14,16},{16,18},{18... | collective-permute-start | bytes 122888 | tf_op jit(solution)/shard_map/ppermute | solution.py:15
  57.3 10.2 %collective-permute-start.3 = (f32[40,256]{1,0:T(8,128)S(1)}, f32[40,256]{1,0:T(8,128)S(1)}, u32[]{:S(2)}, u32[]{:S(2)}) collective-permute-start(f32[40,256]{1,0:T(8,128)S(1)} %bitcast.141), channel_id=1, source_target_pairs={{2,0},{4,2},{6,4},{8,6},{10,8},{12,10},{14,12},{16,14},{18,16},{20... | collective-permute-start | bytes 122888 | tf_op jit(solution)/shard_map/ppermute | solution.py:18
  67.6 2.9 %copy-start.8 = (f32[6,8,8]{2,1,0:T(8,128)S(1)}, f32[6,8,8]{2,1,0:T(8,128)}, u32[]{:S(2)}) copy-start(f32[6,8,8]{2,1,0:T(8,128)} %param.27) | copy-start | bytes 4612
  67.7 2.9 %copy-start.10 = (pred[6,256]{1,0:T(8,128)(4,1)S(1)}, pred[6,256]{1,0:T(8,128)(4,1)}, u32[]{:S(2)}) copy-start(pred[6,256]{1,0:T(8,128)(4,1)} %compare_and_fusion) | copy-start | bytes 4612
  70.3 0.7 copy-start.14
where the time goes:
time: 79.8 us; the launch traced here: 79.1 us
  starting transfers between devices  25 us (31%)
  local copies, waits for them, and re-layouts  22.5 us (28%)
  matrix products  9.77 us (12%)
  blocking collectives  8.62 us (11%)
  waiting for transfers between devices  6.78 us (8%)
  other arithmetic  5.1 us (6%)
  between operations  1.32 us (2%)
    ppermute x2, starting transfers between devices, padded_2(): lax.ppermute(lax.slice_in_dim(block, block.shape[dim] - width, None, axis...  13.4 us
    unnamed x58, local copies, waits for them, and re-layouts  9.13 us
    dot_general x8, matrix products, mult(): return jnp.einsum(form, left, right, precision=HIGH)  8.8 us
    ppermute x2, waiting for transfers between devices, padded_2(): lax.ppermute(lax.slice_in_dim(block, 0, width, axis=dim), axis, backward)  6.77 us
    all_to_all x1, blocking collectives, shards(): lax.all_to_all(second.reshape(nvar * 8, members, scap), 'mem', split_axis...  5.19 us
    all_to_all x1, starting transfers between devices, shards(): lax.all_to_all(to_members, 'mem', split_axis=0, concat_axis=0, tiled=True)  4.03 us
    ppermute x2, starting transfers between devices, padded_2(): lax.ppermute(lax.slice_in_dim(block, 0, width, axis=dim), axis, backward)  4.02 us
    all_to_all x1, starting transfers between devices, shards(): lax.all_to_all(blocks_diag, 'mem', split_axis=1, concat_axis=1, tiled=True)  3.57 us
  transfers between devices with their start and end apart: 6, of which 1 were waited for; matrix products, arithmetic and copies ran while one was open for 31% of the time, Pallas kernels for 0%

commit v1 on v0

v1 whole, which is shorter than its diff:
```python
import functools

import jax
import jax.numpy as jnp
import ml_dtypes
import numpy as np
from jax import lax
from jax.experimental import pallas as pl
from jax.experimental.pallas import tpu as pltpu
from jax.sharding import PartitionSpec as P

MESH = pl.DeviceIdType.MESH
HIGH = lax.Precision.HIGHEST
BF = jnp.bfloat16
F32 = jnp.float32
FAR = 1 << 20


def tables():
    points = np.arange(125)
    coords = [points // 25, points // 5 % 5, points % 5]
    extract = np.zeros((6, 25, 125), np.float32)
    for face in range(6):
        along = face // 2
        others = [c for b, c in enumerate(coords) if b != along]
        index = others[0] * 5 + others[1]
        on_face = coords[along] == 4 * (face % 2)
        extract[face] = (index[None, :] == np.arange(25)[:, None]) & on_face[None, :]
    nodes = -1.0 + 0.5 * np.arange(5)
    basis = np.stack([(1.0 - nodes) / 2.0, (1.0 + nodes) / 2.0], axis=1)
    prolong = np.einsum("ia,jb,kc->ijkabc", basis, basis, basis).reshape(125, 8)
    ext = np.zeros((6, 128, 5, 128), np.float32)
    for v in range(5):
        ext[:, v * 25 : v * 25 + 25, v, :125] = extract
    ext = ext.reshape(768, 640)
    lift = np.ascontiguousarray(ext.T)
    rest = np.zeros((48, 5, 128), np.float32)
    for v in range(5):
        rest[v * 8 : v * 8 + 8, v, :125] = prolong.T
    rest = rest.reshape(48, 640)
    rest_lift = rest @ lift
    pro = np.ascontiguousarray(rest[:40].T)
    pro2 = np.concatenate([pro, pro], axis=1)
    spread = np.zeros((8, 6, 5, 8), np.float32)
    for b in range(8):
        spread[b, :, :, b] = 1.0
    spread = spread.reshape(8, 240)
    gather_a = np.zeros((48, 48), np.float32)
    for v in range(5):
        for f in range(6):
            for a in range(8):
                gather_a[v * 8 + a, f * 8 + a] = 1.0
    same_f = np.zeros((6, 8, 6, 40), np.float32)
    for f in range(6):
        same_f[f, :, f, :] = 1.0
    same_f = same_f.reshape(48, 240)
    same_v = np.zeros((6, 8, 6, 5, 8), np.float32)
    for v in range(5):
        same_v[v, :, :, v, :] = 1.0
    same_v = same_v.reshape(48, 240)
    small = np.zeros((152, 240), np.float32)
    small[0:8] = spread
    small[8:56, :48] = gather_a
    small[56:104] = same_f
    small[104:152] = same_v
    cast = lambda a: np.asarray(a, ml_dtypes.bfloat16)
    return cast(ext), cast(lift), cast(rest), cast(rest_lift), cast(pro2), small


def halves(x):
    hi = x.astype(BF)
    return hi, (x - hi.astype(F32)).astype(BF)


def stacked(x):
    hi = x.astype(BF).astype(F32)
    return jnp.concatenate([hi, x - hi], axis=0).astype(BF)


def dot(a, b):
    return jnp.dot(a, b, preferred_element_type=F32)


def exact(a, b):
    return jnp.dot(a, b, precision=HIGH, preferred_element_type=F32)


def hot(row, base, size):
    places = lax.broadcasted_iota(jnp.int32, (size, row.shape[1]), 0)
    return jnp.where(places == row - base, 1.0, 0.0).astype(BF)


def padded(x):
    return jnp.concatenate([x, jnp.zeros((3, x.shape[1]), F32)], axis=0)


def main_kernel(
    n_grp,
    state, rhs, diag, ext_h, lift_h,
    q_fine, var_mix, mcount, gcount, midx, gidx, fsrc, cdiag, q_coarse, g_coarse, owner, cnbr,
    rest, rest_lift, small,
    resid_out, second_out,
    st, rh, dg, ext, lift, uh, ul, qs,
    ohs, tr, snd_g, snd_m, snd_n, rcv_g, rcv_m, rcv_n,
    ohr, nlh, nll, resl, ohc, st_hot, blks, mine, rim, resv,
    in_sem, snd_sem, rcv_sem, out_sem,
):
    g = lax.axis_index("grp")
    m = lax.axis_index("mem")
    other = 1 - m
    prev = lax.rem(g + n_grp - 1, n_grp)
    nxt = lax.rem(g + 1, n_grp)

    loads = [
        pltpu.make_async_copy(state, st, in_sem.at[0]),
        pltpu.make_async_copy(ext_h, ext, in_sem.at[1]),
        pltpu.make_async_copy(rhs, rh, in_sem.at[2]),
        pltpu.make_async_copy(diag, dg, in_sem.at[3]),
        pltpu.make_async_copy(lift_h, lift, in_sem.at[4]),
    ]
    for c in loads:
        c.start()

    barrier = pltpu.get_barrier_semaphore()
    near_devices = [(prev, 0), (prev, 1), (nxt, 0), (nxt, 1), (g, other)]
    for d in near_devices:
        pl.semaphore_signal(barrier, inc=1, device_id=d, device_id_type=MESH)

    lane_g = lax.broadcasted_iota(jnp.int32, (1, 256), 1)
    lane_m = lax.broadcasted_iota(jnp.int32, (1, 128), 1)
    for t in range(2):
        row = jnp.where(lane_g < gcount[0, t], gidx[0, t : t + 1, :], -1)
        ohs[:, t * 256 : t * 256 + 256] = hot(row, 0, 1536)
    mrow = jnp.where(m == 0, midx[0, 1:2, :], midx[0, 0:1, :])
    mlim = jnp.where(m == 0, mcount[0, 1], mcount[0, 0])
    ohs[:, 512:640] = hot(jnp.where(lane_m < mlim, mrow, -1), 0, 1536)
    nbr = cnbr[...]
    snd_n[0:6, :] = jnp.where(m == 0, nbr[:, 128:256], nbr[:, 0:128])
    snd_n[6:8, :] = jnp.zeros((2, 128), jnp.int32)

    loads[0].wait()
    for v in range(5):
        hi, lo = halves(padded(st[v]))
        uh[v * 128 : v * 128 + 128, :] = hi
        ul[v * 128 : v * 128 + 128, :] = lo
    loads[1].wait()
    for f in range(6):
        e = ext[f * 128 : f * 128 + 128, :]
        tr[0:128, f * 256 : f * 256 + 256] = dot(e, uh[...]).astype(BF)
        tr[128:256, f * 256 : f * 256 + 256] = dot(e, ul[...]).astype(BF)

    def remote(src, dst, i, j, device):
        return pltpu.make_async_remote_copy(
            src_ref=src, dst_ref=dst, send_sem=snd_sem.at[i], recv_sem=rcv_sem.at[j],
            device_id=device, device_id_type=MESH,
        )

    pl.semaphore_wait(barrier, 5)
    c_nbr = remote(snd_n, rcv_n, 0, 0, (g, other))
    c_nbr.start()
    picked = dot(tr[...], ohs[:, 0:256])
    snd_g[0] = picked[:128] + picked[128:]
    c_prev = remote(snd_g.at[0], rcv_g.at[1], 1, 1, (prev, m))
    c_prev.start()
    picked = dot(tr[...], ohs[:, 256:512])
    snd_g[1] = picked[:128] + picked[128:]
    c_next = remote(snd_g.at[1], rcv_g.at[0], 2, 2, (nxt, m))
    c_next.start()
    picked = dot(tr[...], ohs[:, 512:640])
    snd_m[...] = picked[:128] + picked[128:]
    c_mem = remote(snd_m, rcv_m, 3, 3, (g, other))
    c_mem.start()

    base_prev = jnp.where(g == 0, FAR, 1792)
    base_next = jnp.where(g == n_grp - 1, FAR, 2048)
    base_mem = 1536 + other * 128

    def local_faces(f, carry):
        row = fsrc[pl.ds(f, 1), :]
        acc = dot(tr[...], hot(row, 0, 1536))
        at = pl.multiple_of(f * 128, 128)
        nlh[pl.ds(at, 128), :] = acc[:128].astype(BF)
        nll[pl.ds(at, 128), :] = acc[128:].astype(BF)
        ohr[f, 0:256, :] = hot(row, base_prev, 256)
        ohr[f, 256:512, :] = hot(row, base_next, 256)
        ohr[f, 512:640, :] = hot(row, base_mem, 128)
        return carry

    lax.fori_loop(0, 6, local_faces, 0)

    qs[...] = jnp.zeros((128, 128), F32)
    qs[0:125, 0:125] = q_fine[...]
    qh, ql = halves(qs[...])
    loads[2].wait()
    loads[3].wait()
    for v in range(5):
        total = dot(qh, uh[v * 128 : v * 128 + 128, :]) + dot(qh, ul[v * 128 : v * 128 + 128, :])
        total = (total + dot(ql, uh[v * 128 : v * 128 + 128, :]))[:125]
        total = total + dg[v] * st[v]
        for w in range(5):
            total = total + var_mix[v, w] * st[w]
        resl[v * 128 : v * 128 + 128, :] = padded(rh[v] - total)
    rl_h, rl_l = halves(resl[...])
    rest0 = dot(rest[...], rl_h) + dot(rest[...], rl_l)
    rest0 = rest0 + dot(rest_lift[...], nlh[...]) + dot(rest_lift[...], nll[...])

    own = owner[...].astype(F32)
    before = lax.broadcasted_iota(jnp.int32, (256, 256), 0) < lax.broadcasted_iota(jnp.int32, (256, 256), 1)
    ones_before = dot(jnp.broadcast_to(own, (16, 256)).astype(BF), jnp.where(before, 1.0, 0.0).astype(BF))[0:1]
    ones_before = ones_before.astype(jnp.int32)
    target = jnp.where(owner[...] == 1, 128 + ones_before, lane_g - ones_before)
    st_hot[...] = hot(target, 0, 256)

    gfa = g_coarse[...]
    gg = exact(gfa, small[0:8, :]) * small[56:104, :]
    gg = exact(small[8:56, 0:48], gg) * small[104:152, :]
    ggh, ggl = halves(gg)
    qrep = jnp.concatenate([q_coarse[...]] * 5, axis=0)
    qq = exact(qrep, small[0:8, 0:40]) * small[104:144, 0:40]

    c_prev.wait_recv()
    c_next.wait_recv()
    c_mem.wait_recv()
    parts = []
    for ref in (rcv_g.at[0], rcv_g.at[1], rcv_m):
        hi, lo = halves(ref[...])
        parts.append(jnp.concatenate([hi, lo], axis=0))
    for f in range(6):
        acc = dot(parts[0], ohr[f, 0:256, :]) + dot(parts[1], ohr[f, 256:512, :]) + dot(parts[2], ohr[f, 512:640, :])
        nh, nl = acc[:128].astype(BF), acc[128:].astype(BF)
        rlf = rest_lift[:, f * 128 : f * 128 + 128]
        rest0 = rest0 + dot(rlf, nh) + dot(rlf, nl)
        nlh[f * 128 : f * 128 + 128, :] += nh
        nll[f * 128 : f * 128 + 128, :] += nl
    cd = cdiag[...]
    first = (0.8 * 0.064) * rest0[:40] / cd
    packed = lax.dot_general(stacked(first), st_hot[...], (((1,), (1,)), ((), ())), preferred_element_type=F32)
    mine[...] = packed[:40] + packed[40:]
    c_two = []
    for i, (d, place) in enumerate(
        [((prev, 0), 4 + m), ((prev, 1), 4 + m), ((nxt, 0), m), ((nxt, 1), m), ((g, other), 2 + m)]
    ):
        c = remote(mine, blks.at[place], 4 + i, 4 + place, d)
        c.start()
        c_two.append(c)

    for v in range(5):
        lf = lift[v * 128 : v * 128 + 128, :]
        if v == 0:
            loads[4].wait()
            lf = lift[0:128, :]
        full = resl[v * 128 : v * 128 + 128, :] + dot(lf, nlh[...]) + dot(lf, nll[...])
        resv[v] = full[:125]
    c_out = pltpu.make_async_copy(resv, resid_out, out_sem)
    c_out.start()
    inner = exact(qq, first)
    weight = 0.8 / cd
    base = 1.2 * first - weight * inner

    c_nbr.wait_recv()
    own_nbr = jnp.where(m == 0, nbr[:, 0:128], nbr[:, 128:256])
    got_nbr = rcv_n[0:6, :]
    for o in range(2):
        lists = jnp.where(m == o, own_nbr, got_nbr)
        lists = jnp.where((g == 0) & (lists < 256), FAR, lists)
        lists = jnp.where((g == n_grp - 1) & (lists >= 512), FAR, lists)
        for f in range(6):
            ohc[o, :, f * 128 : f * 128 + 128] = hot(lists[f : f + 1, :], 0, 768)

    def arrived(place):
        remote(mine, blks.at[place], 4, 4 + place, (g, other)).wait_recv()

    for place in (2 + other, 0, 1, 4, 5):
        arrived(place)
    blks[2 + m] = mine[...]
    for j in range(6):
        both = stacked(blks[j])
        rim[0, :, j * 128 : j * 128 + 128] = both[:, 0:128]
        rim[1, :, j * 128 : j * 128 + 128] = both[:, 128:256]
    nhs, nls = [], []
    for o in range(2):
        near = dot(rim[o], ohc[o])
        nhs.append(jnp.concatenate([near[:40, f * 128 : f * 128 + 128] for f in range(6)], axis=0))
        nls.append(jnp.concatenate([near[40:, f * 128 : f * 128 + 128] for f in range(6)], axis=0))
    nh = jnp.concatenate(nhs, axis=1).astype(BF)
    nl = jnp.concatenate(nls, axis=1).astype(BF)
    across = (dot(ggh, nh) + dot(ggh, nl) + dot(ggl, nh))[:40]
    back = dot(stacked(across), st_hot[...])
    second_out[...] = base + weight * (back[:40] + back[40:])

    for c in [c_nbr, c_prev, c_next, c_mem] + c_two:
        c.wait_send()
    c_out.wait()


def last_kernel(resid, second, pro2, resid_out, corr_out, corr, sem):
    c0 = pltpu.make_async_copy(resid, resid_out, sem.at[0])
    c0.start()
    both = stacked(second[...])
    copies = []
    for v in range(5):
        corr[v] = dot(pro2[v * 128 : v * 128 + 128, :], both)[:125]
        c = pltpu.make_async_copy(corr.at[v], corr_out.at[v], sem.at[1 + v])
        c.start()
        copies.append(c)
    c0.wait()
    for c in copies:
        c.wait()


def shards(
    state, rhs, fine_diag, q_fine, var_mix, mem_count, grp_count, send_mem_idx, send_grp_idx,
    face_src, coarse_diag, q_coarse, g_coarse, owner, coarse_nbr,
):
    ext, lift, rest, rest_lift, pro2, small = tables()
    n_grp = lax.axis_size("grp")
    hbm = pl.BlockSpec(memory_space=pl.ANY)
    vmem = pl.BlockSpec(memory_space=pltpu.VMEM)
    smem = pl.BlockSpec(memory_space=pltpu.SMEM)
    field = jax.ShapeDtypeStruct((5, 125, 256), F32)
    resid, second = pl.pallas_call(
        functools.partial(main_kernel, n_grp),
        out_shape=(field, jax.ShapeDtypeStruct((40, 256), F32)),
        in_specs=[hbm] * 5 + [vmem, smem, smem, smem] + [vmem] * 11,
        out_specs=(hbm, vmem),
        scratch_shapes=[
            pltpu.VMEM((5, 125, 256), F32),
            pltpu.VMEM((5, 125, 256), F32),
            pltpu.VMEM((5, 125, 256), F32),
            pltpu.VMEM((768, 640), BF),
            pltpu.VMEM((640, 768), BF),
            pltpu.VMEM((640, 256), BF),
            pltpu.VMEM((640, 256), BF),
            pltpu.VMEM((128, 128), F32),
            pltpu.VMEM((1536, 640), BF),
            pltpu.VMEM((256, 1536), BF),
            pltpu.VMEM((2, 128, 256), F32),
            pltpu.VMEM((128, 128), F32),
            pltpu.VMEM((8, 128), jnp.int32),
            pltpu.VMEM((2, 128, 256), F32),
            pltpu.VMEM((128, 128), F32),
            pltpu.VMEM((8, 128), jnp.int32),
            pltpu.VMEM((6, 640, 256), BF),
            pltpu.VMEM((768, 256), BF),
            pltpu.VMEM((768, 256), BF),
            pltpu.VMEM((640, 256), F32),
            pltpu.VMEM((2, 768, 768), BF),
            pltpu.VMEM((256, 256), BF),
            pltpu.VMEM((6, 40, 256), F32),
            pltpu.VMEM((40, 256), F32),
            pltpu.VMEM((2, 80, 768), BF),
            pltpu.VMEM((5, 125, 256), F32),
            pltpu.SemaphoreType.DMA((5,)),
            pltpu.SemaphoreType.DMA((9,)),
            pltpu.SemaphoreType.DMA((10,)),
            pltpu.SemaphoreType.DMA,
        ],
        compiler_params=pltpu.CompilerParams(
            collective_id=0, has_side_effects=True, vmem_limit_bytes=40 * 1024 * 1024
        ),
        name="residual_and_sweeps",
    )(
        state, rhs, fine_diag, jnp.asarray(ext), jnp.asarray(lift),
        q_fine, var_mix, mem_count, grp_count, send_mem_idx, send_grp_idx, face_src,
        coarse_diag.reshape(40, 256), q_coarse, g_coarse.reshape(48, 8), owner.reshape(1, 256), coarse_nbr,
        jnp.asarray(rest), jnp.asarray(rest_lift), jnp.asarray(small),
    )
    return pl.pallas_call(
        last_kernel,
        out_shape=(field, field),
        in_specs=[hbm, vmem, vmem],
        out_specs=(hbm, hbm),
        scratch_shapes=[pltpu.VMEM((5, 125, 256), F32), pltpu.SemaphoreType.DMA((6,))],
        compiler_params=pltpu.CompilerParams(vmem_limit_bytes=16 * 1024 * 1024),
        name="prolongation",
    )(resid, second, jnp.asarray(pro2))


def solution(mesh):
    whole = ("grp", "mem")
    return jax.shard_map(
        shards,
        mesh=mesh,
        in_specs=(
            P(None, None, whole), P(None, None, whole), P(None, None, whole), P(), P(),
            P(whole, None), P(whole, None), P(whole, None, None), P(whole, None, None), P(None, whole),
            P(None, None, whole), P(), P(), P(whole, None), P(None, whole),
        ),
        out_specs=(P(None, None, whole), P(None, None, whole)),
        check_vma=False,
    )
```

time: 79.8 us -> 52.6 us (0.66)
  the two profiles are of different devices: /device:TPU:255 before, /device:TPU:1 now
where the time goes in v1:
time: 52.6 us; the launch traced here: 51.8 us
  Pallas kernels  35.7 us (68%)
  local copies, waits for them, and re-layouts  15.4 us (29%)
  between operations  0.7 us (1%)
    pallas_call x1, Pallas kernels, shards(): pl.pallas_call(functools.partial(main_kernel, n_grp), out_shape=(field, j...  34.6 us
    unnamed x42, local copies, waits for them, and re-layouts  15.4 us
    pallas_call x1, Pallas kernels, shards(): pl.pallas_call(last_kernel, out_shape=(field, field), in_specs=[hbm, vmem...  1.1 us

profile of v1, /device:TPU:1, one launch (start us, length us, event | category | flops | bytes accessed | tf_op | source)
XLA Modules:
  0.0 51.8 jit_solution(4294001895444530481)
XLA Ops:
  0.6 0.0 copy-start.14
  0.6 0.0 copy-start.17
  0.7 0.0 copy-start.19
  0.7 0.7 %copy-done.14 = f32[5,5]{1,0:T(8,128)S(1)} copy-done((f32[5,5]{1,0:T(8,128)S(1)}, f32[5,5]{1,0:T(8,128)}, u32[]{:S(2)}) %copy-start.14) | copy-done | bytes 124
  1.3 0.0 copy-done.17
  1.3 0.0 copy-done.19
  1.3 0.0 copy-start
  1.3 1.2 %copy-done = bf16[640,768]{1,0:T(8,128)(2,1)S(1)} copy-done((bf16[640,768]{1,0:T(8,128)(2,1)S(1)}, bf16[640,768]{1,0:T(8,128)(2,1)}, u32[]{:S(2)}) %copy-start) | copy-done | bytes 983064
  2.5 0.0 copy-start.1
  2.5 1.2 %copy-done.1 = bf16[768,640]{1,0:T(8,128)(2,1)S(1)} copy-done((bf16[768,640]{1,0:T(8,128)(2,1)S(1)}, bf16[768,640]{1,0:T(8,128)(2,1)}, u32[]{:S(2)}) %copy-start.1) | copy-done | bytes 983064
  3.7 0.0 copy-start.2
  3.7 1.1 %copy-done.2 = f32[5,125,256]{2,1,0:T(8,128)S(1)} copy-done((f32[5,125,256]{2,1,0:T(8,128)S(1)}, f32[5,125,256]{2,1,0:T(8,128)}, u32[]{:S(2)}) %copy-start.2) | copy-done | bytes 640024
  4.8 0.0 copy-start.3
  4.8 1.1 %copy-done.3 = f32[5,125,256]{2,1,0:T(8,128)S(1)} copy-done((f32[5,125,256]{2,1,0:T(8,128)S(1)}, f32[5,125,256]{2,1,0:T(8,128)}, u32[]{:S(2)}) %copy-start.3) | copy-done | bytes 640024
  5.9 0.0 copy-start.4
  5.9 1.1 %copy-done.4 = f32[5,125,256]{2,1,0:T(8,128)S(1)} copy-done((f32[5,125,256]{2,1,0:T(8,128)S(1)}, f32[5,125,256]{2,1,0:T(8,128)}, u32[]{:S(2)}) %copy-start.4) | copy-done | bytes 640024
  7.0 0.0 copy-start.6
  7.0 0.9 %copy-done.6 = f32[152,240]{1,0:T(8,128)S(1)} copy-done((f32[152,240]{1,0:T(8,128)S(1)}, f32[152,240]{1,0:T(8,128)}, u32[]{:S(2)}) %copy-start.6) | copy-done | bytes 145944
  7.9 0.0 copy-start.7
  7.9 0.9 %copy-done.7 = bf16[48,768]{1,0:T(8,128)(2,1)S(1)} copy-done((bf16[48,768]{1,0:T(8,128)(2,1)S(1)}, bf16[48,768]{1,0:T(8,128)(2,1)}, u32[]{:S(2)}) %copy-start.7) | copy-done | bytes 73752
  8.8 0.0 copy-start.8
  8.8 0.8 %copy-done.8 = f32[125,125]{1,0:T(8,128)S(1)} copy-done((f32[125,125]{1,0:T(8,128)S(1)}, f32[125,125]{1,0:T(8,128)}, u32[]{:S(2)}) %copy-start.8) | copy-done | bytes 62524
  9.6 0.0 copy-start.9
  9.6 0.8 %copy-done.9 = bf16[48,640]{1,0:T(8,128)(2,1)S(1)} copy-done((bf16[48,640]{1,0:T(8,128)(2,1)S(1)}, bf16[48,640]{1,0:T(8,128)(2,1)}, u32[]{:S(2)}) %copy-start.9) | copy-done | bytes 61464
  10.5 0.0 copy-start.10
  10.5 0.8 %copy-done.10 = f32[5,8,256]{2,1,0:T(8,128)S(1)} copy-done((f32[5,8,256]{2,1,0:T(8,128)S(1)}, f32[5,8,256]{2,1,0:T(8,128)}, u32[]{:S(2)}) %copy-start.10) | copy-done | bytes 40984
  11.2 0.0 copy-start.11
  11.3 0.7 %copy-done.11 = f32[6,8,8]{2,1,0:T(8,128)S(1)} copy-done((f32[6,8,8]{2,1,0:T(8,128)S(1)}, f32[6,8,8]{2,1,0:T(8,128)}, u32[]{:S(2)}) %copy-start.11) | copy-done | bytes 1560
  12.0 0.0 copy-start.12
  12.0 0.7 %copy-done.12 = s32[6,256]{1,0:T(8,128)S(1)} copy-done((s32[6,256]{1,0:T(8,128)S(1)}, s32[6,256]{1,0:T(8,128)}, u32[]{:S(2)}) %copy-start.12) | copy-done | bytes 6168
  12.7 0.0 copy-start.13
  12.7 0.7 %copy-done.13 = s32[6,256]{1,0:T(8,128)S(1)} copy-done((s32[6,256]{1,0:T(8,128)S(1)}, s32[6,256]{1,0:T(8,128)}, u32[]{:S(2)}) %copy-start.13) | copy-done | bytes 6168
  13.4 0.0 copy-start.15
  13.4 0.7 %copy-done.15 = f32[8,8]{1,0:T(8,128)S(1)} copy-done((f32[8,8]{1,0:T(8,128)S(1)}, f32[8,8]{1,0:T(8,128)}, u32[]{:S(2)}) %copy-start.15) | copy-done | bytes 280
  14.1 0.0 copy-start.16
  14.1 0.7 %copy-done.16 = s32[1,2,256]{2,1,0:T(2,128)S(1)} copy-done((s32[1,2,256]{2,1,0:T(2,128)S(1)}, s32[1,2,256]{2,1,0:T(2,128)}, u32[]{:S(2)}) %copy-start.16) | copy-done | bytes 2072
  14.8 0.0 copy-start.18
  14.8 0.7 %copy-done.18 = s32[256,1]{0,1:T(1,128)S(1)} copy-done((s32[256,1]{0,1:T(1,128)S(1)}, s32[256,1]{0,1:T(1,128)}, u32[]{:S(2)}) %copy-start.18) | copy-done | bytes 1048
  15.4 0.0 copy-start.20
  15.4 0.7 %copy-done.20 = s32[1,2]{1,0:T(1,128)S(1)} copy-done((s32[1,2]{1,0:T(1,128)S(1)}, s32[1,2]{1,0:T(1,128)}, u32[]{:S(2)}) %copy-start.20) | copy-done | bytes 32
  16.1 0.0 copy-start.5
  16.1 34.6 %residual_and_sweeps.1 = (f32[5,125,256]{2,1,0:T(8,128)S(1)}, f32[40,256]{1,0:T(8,128)S(1)}) custom-call(f32[5,125,256]{2,1,0:T(8,128)S(1)} %copy-done.2, f32[5,125,256]{2,1,0:T(8,128)S(1)} %copy-done.3, f32[5,125,256]{2,1,0:T(8,128)S(1)} %copy-done.4, bf16[768,640]{1,0:T(8,128)(2,1)S(1)} %copy-done.1, bf16[640,768]{1,0:T(8,128)(2,1)S(1)} %copy-done, ...), custom_call_target="tpu_custom_call" | custom-call | tf_op jit(solution)/shard_map/residual_and_sweeps/pallas_call | solution.py:321
  50.7 0.0 copy-done.5
  50.7 1.1 %prolongation.1 = (f32[5,125,256]{2,1,0:T(8,128)}, f32[5,125,256]{2,1,0:T(8,128)}) custom-call(f32[5,125,256]{2,1,0:T(8,128)S(1)} %get-tuple-element.4.resid, f32[40,256]{1,0:T(8,128)S(1)} %get-tuple-element.5.second, bf16[640,80]{1,0:T(8,128)(2,1)S(1)} %copy-done.5), custom_call_target="tpu_custom_call" | custom-call | tf_op jit(solution)/shard_map/prolongation/pallas_call | solution.py:368
Async XLA Ops:
  0.6 0.7 %copy-start.14 = (f32[5,5]{1,0:T(8,128)S(1)}, f32[5,5]{1,0:T(8,128)}, u32[]{:S(2)}) copy-start(f32[5,5]{1,0:T(8,128)} %var_mix.1) | copy-start | bytes 304
  0.6 0.7 %copy-start.17 = (s32[1,2,128]{2,1,0:T(2,128)S(1)}, s32[1,2,128]{2,1,0:T(2,128)}, u32[]{:S(2)}) copy-start(s32[1,2,128]{2,1,0:T(2,128)} %midx.1) | copy-start | bytes 3076
  0.7 0.7 %copy-start.19 = (s32[1,2]{1,0:T(1,128)S(1)}, s32[1,2]{1,0:T(1,128)}, u32[]{:S(2)}) copy-start(s32[1,2]{1,0:T(1,128)} %mcount.1) | copy-start | bytes 28
  1.3 1.2 %copy-start = (bf16[640,768]{1,0:T(8,128)(2,1)S(1)}, bf16[640,768]{1,0:T(8,128)(2,1)}, u32[]{:S(2)}) copy-start(bf16[640,768]{1,0:T(8,128)(2,1)} %constant.13.clone.lift_h) | copy-start | bytes 2949124
  2.5 1.2 %copy-start.1 = (bf16[768,640]{1,0:T(8,128)(2,1)S(1)}, bf16[768,640]{1,0:T(8,128)(2,1)}, u32[]{:S(2)}) copy-start(bf16[768,640]{1,0:T(8,128)(2,1)} %constant.12.clone.ext_h) | copy-start | bytes 2949124
  3.7 1.1 %copy-start.2 = (f32[5,125,256]{2,1,0:T(8,128)S(1)}, f32[5,125,256]{2,1,0:T(8,128)}, u32[]{:S(2)}) copy-start(f32[5,125,256]{2,1,0:T(8,128)} %state.1) | copy-start | bytes 1920004
  4.8 1.1 %copy-start.3 = (f32[5,125,256]{2,1,0:T(8,128)S(1)}, f32[5,125,256]{2,1,0:T(8,128)}, u32[]{:S(2)}) copy-start(f32[5,125,256]{2,1,0:T(8,128)} %rhs.1) | copy-start | bytes 1920004
  5.9 1.1 %copy-start.4 = (f32[5,125,256]{2,1,0:T(8,128)S(1)}, f32[5,125,256]{2,1,0:T(8,128)}, u32[]{:S(2)}) copy-start(f32[5,125,256]{2,1,0:T(8,128)} %diag.1) | copy-start | bytes 1920004
  7.0 0.9 %copy-start.6 = (f32[152,240]{1,0:T(8,128)S(1)}, f32[152,240]{1,0:T(8,128)}, u32[]{:S(2)}) copy-start(f32[152,240]{1,0:T(8,128)} %constant.16.clone.small) | copy-start | bytes 437764
  7.9 0.9 %copy-start.7 = (bf16[48,768]{1,0:T(8,128)(2,1)S(1)}, bf16[48,768]{1,0:T(8,128)(2,1)}, u32[]{:S(2)}) copy-start(bf16[48,768]{1,0:T(8,128)(2,1)} %constant.15.clone.rest_lift) | copy-start | bytes 221188
  8.8 0.8 %copy-start.8 = (f32[125,125]{1,0:T(8,128)S(1)}, f32[125,125]{1,0:T(8,128)}, u32[]{:S(2)}) copy-start(f32[125,125]{1,0:T(8,128)} %q_fine.1) | copy-start | bytes 187504
  9.6 0.8 %copy-start.9 = (bf16[48,640]{1,0:T(8,128)(2,1)S(1)}, bf16[48,640]{1,0:T(8,128)(2,1)}, u32[]{:S(2)}) copy-start(bf16[48,640]{1,0:T(8,128)(2,1)} %constant.14.clone.rest) | copy-start | bytes 184324
  10.5 0.8 %copy-start.10 = (f32[5,8,256]{2,1,0:T(8,128)S(1)}, f32[5,8,256]{2,1,0:T(8,128)}, u32[]{:S(2)}) copy-start(f32[5,8,256]{2,1,0:T(8,128)} %param.31) | copy-start | bytes 122884
  11.2 0.7 %copy-start.11 = (f32[6,8,8]{2,1,0:T(8,128)S(1)}, f32[6,8,8]{2,1,0:T(8,128)}, u32[]{:S(2)}) copy-start(f32[6,8,8]{2,1,0:T(8,128)} %param.33) | copy-start | bytes 4612
  12.0 0.7 %copy-start.12 = (s32[6,256]{1,0:T(8,128)S(1)}, s32[6,256]{1,0:T(8,128)}, u32[]{:S(2)}) copy-start(s32[6,256]{1,0:T(8,128)} %fsrc.1) | copy-start | bytes 18436
  12.7 0.7 %copy-start.13 = (s32[6,256]{1,0:T(8,128)S(1)}, s32[6,256]{1,0:T(8,128)}, u32[]{:S(2)}) copy-start(s32[6,256]{1,0:T(8,128)} %cnbr.1) | copy-start | bytes 18436
  13.4 0.7 %copy-start.15 = (f32[8,8]{1,0:T(8,128)S(1)}, f32[8,8]{1,0:T(8,128)}, u32[]{:S(2)}) copy-start(f32[8,8]{1,0:T(8,128)} %q_coarse.1) | copy-start | bytes 772
  14.1 0.7 %copy-start.16 = (s32[1,2,256]{2,1,0:T(2,128)S(1)}, s32[1,2,256]{2,1,0:T(2,128)}, u32[]{:S(2)}) copy-start(s32[1,2,256]{2,1,0:T(2,128)} %gidx.1) | copy-start | bytes 6148
  14.8 0.7 %copy-start.18 = (s32[256,1]{0,1:T(1,128)S(1)}, s32[256,1]{0,1:T(1,128)}, u32[]{:S(2)}) copy-start(s32[256,1]{0,1:T(1,128)} %param.34) | copy-start | bytes 3076
  15.4 0.7 %copy-start.20 = (s32[1,2]{1,0:T(1,128)S(1)}, s32[1,2]{1,0:T(1,128)}, u32[]{:S(2)}) copy-start(s32[1,2]{1,0:T(1,128)} %gcount.1) | copy-start | bytes 28
  16.1 34.6 %copy-start.5 = (bf16[640,80]{1,0:T(8,128)(2,1)S(1)}, bf16[640,80]{1,0:T(8,128)(2,1)}, u32[]{:S(2)}) copy-start(bf16[640,80]{1,0:T(8,128)(2,1)} %constant.17.clone.pro2) | copy-start | bytes 307204

commit v2 on v1

--- a/solution.py
+++ b/solution.py
@@ -94,30 +94,25 @@
     return jnp.concatenate([x, jnp.zeros((3, x.shape[1]), F32)], axis=0)
 
 
-def main_kernel(
-    n_grp,
-    state, rhs, diag, ext_h, lift_h,
-    q_fine, var_mix, mcount, gcount, midx, gidx, fsrc, cdiag, q_coarse, g_coarse, owner, cnbr,
-    rest, rest_lift, small,
-    resid_out, second_out,
-    st, rh, dg, ext, lift, uh, ul, qs,
-    ohs, tr, snd_g, snd_m, snd_n, rcv_g, rcv_m, rcv_n,
-    ohr, nlh, nll, resl, ohc, st_hot, blks, mine, rim, resv,
-    in_sem, snd_sem, rcv_sem, out_sem,
-):
+def main_kernel(n_grp, *refs):
+    sources, (resid_out, second_out), scratch = refs[:20], refs[20:22], refs[22:]
+    (
+        st, midx, gidx, mcount, gcount, ext, cnbr, fsrc, rh, dg, q_fine, var_mix,
+        rest, rest_lift, owner, cdiag, g_coarse, q_coarse, small, lift,
+    ) = scratch[:20]
+    (
+        uh, ul, qs,
+        ohs, tr, snd_g, snd_m, snd_n, rcv_g, rcv_m, rcv_n,
+        ohr, nlh, nll, resl, ohc, st_hot, blks, mine, rim, resv, mine2,
+        in_sem, snd_sem, rcv_sem, out_sem,
+    ) = scratch[20:]
     g = lax.axis_index("grp")
     m = lax.axis_index("mem")
     other = 1 - m
     prev = lax.rem(g + n_grp - 1, n_grp)
     nxt = lax.rem(g + 1, n_grp)
 
-    loads = [
-        pltpu.make_async_copy(state, st, in_sem.at[0]),
-        pltpu.make_async_copy(ext_h, ext, in_sem.at[1]),
-        pltpu.make_async_copy(rhs, rh, in_sem.at[2]),
-        pltpu.make_async_copy(diag, dg, in_sem.at[3]),
-        pltpu.make_async_copy(lift_h, lift, in_sem.at[4]),
-    ]
+    loads = [pltpu.make_async_copy(src, scratch[i], in_sem.at[i]) for i, src in enumerate(sources)]
     for c in loads:
         c.start()
 
@@ -126,13 +121,15 @@
     for d in near_devices:
         pl.semaphore_signal(barrier, inc=1, device_id=d, device_id_type=MESH)
 
+    for i in (1, 2, 3, 4, 6):
+        loads[i].wait()
     lane_g = lax.broadcasted_iota(jnp.int32, (1, 256), 1)
     lane_m = lax.broadcasted_iota(jnp.int32, (1, 128), 1)
     for t in range(2):
-        row = jnp.where(lane_g < gcount[0, t], gidx[0, t : t + 1, :], -1)
+        row = jnp.where(lane_g < gcount[0:1, t : t + 1], gidx[0, t : t + 1, :], -1)
         ohs[:, t * 256 : t * 256 + 256] = hot(row, 0, 1536)
     mrow = jnp.where(m == 0, midx[0, 1:2, :], midx[0, 0:1, :])
-    mlim = jnp.where(m == 0, mcount[0, 1], mcount[0, 0])
+    mlim = jnp.where(m == 0, mcount[0:1, 1:2], mcount[0:1, 0:1])
     ohs[:, 512:640] = hot(jnp.where(lane_m < mlim, mrow, -1), 0, 1536)
     nbr = cnbr[...]
     snd_n[0:6, :] = jnp.where(m == 0, nbr[:, 128:256], nbr[:, 0:128])
@@ -143,7 +140,7 @@
         hi, lo = halves(padded(st[v]))
         uh[v * 128 : v * 128 + 128, :] = hi
         ul[v * 128 : v * 128 + 128, :] = lo
-    loads[1].wait()
+    loads[5].wait()
     for f in range(6):
         e = ext[f * 128 : f * 128 + 128, :]
         tr[0:128, f * 256 : f * 256 + 256] = dot(e, uh[...]).astype(BF)
@@ -186,19 +183,20 @@
         ohr[f, 512:640, :] = hot(row, base_mem, 128)
         return carry
 
+    loads[7].wait()
     lax.fori_loop(0, 6, local_faces, 0)
 
+    for i in range(8, 19):
+        loads[i].wait()
     qs[...] = jnp.zeros((128, 128), F32)
     qs[0:125, 0:125] = q_fine[...]
     qh, ql = halves(qs[...])
-    loads[2].wait()
-    loads[3].wait()
     for v in range(5):
         total = dot(qh, uh[v * 128 : v * 128 + 128, :]) + dot(qh, ul[v * 128 : v * 128 + 128, :])
         total = (total + dot(ql, uh[v * 128 : v * 128 + 128, :]))[:125]
         total = total + dg[v] * st[v]
         for w in range(5):
-            total = total + var_mix[v, w] * st[w]
+            total = total + var_mix[v : v + 1, w : w + 1] * st[w]
         resl[v * 128 : v * 128 + 128, :] = padded(rh[v] - total)
     rl_h, rl_l = halves(resl[...])
     rest0 = dot(rest[...], rl_h) + dot(rest[...], rl_l)
@@ -247,11 +245,11 @@
     for v in range(5):
         lf = lift[v * 128 : v * 128 + 128, :]
         if v == 0:
-            loads[4].wait()
+            loads[19].wait()
             lf = lift[0:128, :]
         full = resl[v * 128 : v * 128 + 128, :] + dot(lf, nlh[...]) + dot(lf, nll[...])
         resv[v] = full[:125]
-    c_out = pltpu.make_async_copy(resv, resid_out, out_sem)
+    c_out = pltpu.make_async_copy(resv, resid_out, out_sem.at[0])
     c_out.start()
     inner = exact(qq, first)
     weight = 0.8 / cd
@@ -286,24 +284,31 @@
     nl = jnp.concatenate(nls, axis=1).astype(BF)
     across = (dot(ggh, nh) + dot(ggh, nl) + dot(ggl, nh))[:40]
     back = dot(stacked(across), st_hot[...])
-    second_out[...] = base + weight * (back[:40] + back[40:])
+    mine2[...] = base + weight * (back[:40] + back[40:])
+    c_second = pltpu.make_async_copy(mine2, second_out, out_sem.at[1])
+    c_second.start()
 
     for c in [c_nbr, c_prev, c_next, c_mem] + c_two:
         c.wait_send()
     c_out.wait()
-
-
-def last_kernel(resid, second, pro2, resid_out, corr_out, corr, sem):
-    c0 = pltpu.make_async_copy(resid, resid_out, sem.at[0])
-    c0.start()
+    c_second.wait()
+
+
+def last_kernel(resid, second_h, pro2_h, resid_out, corr_out, second, pro2, corr, sem):
+    loads = [pltpu.make_async_copy(second_h, second, sem.at[0]), pltpu.make_async_copy(pro2_h, pro2, sem.at[1])]
+    whole = pltpu.make_async_copy(resid, resid_out, sem.at[2])
+    for c in loads:
+        c.start()
+    whole.start()
+    for c in loads:
+        c.wait()
     both = stacked(second[...])
-    copies = []
+    copies = [whole]
     for v in range(5):
         corr[v] = dot(pro2[v * 128 : v * 128 + 128, :], both)[:125]
-        c = pltpu.make_async_copy(corr.at[v], corr_out.at[v], sem.at[1 + v])
+        c = pltpu.make_async_copy(corr.at[v], corr_out.at[v], sem.at[3 + v])
         c.start()
         copies.append(c)
-    c0.wait()
     for c in copies:
         c.wait()
 
@@ -314,21 +319,20 @@
 ):
     ext, lift, rest, rest_lift, pro2, small = tables()
     n_grp = lax.axis_size("grp")
-    hbm = pl.BlockSpec(memory_space=pl.ANY)
-    vmem = pl.BlockSpec(memory_space=pltpu.VMEM)
-    smem = pl.BlockSpec(memory_space=pltpu.SMEM)
+    hbm = pl.BlockSpec(memory_space=pltpu.HBM)
     field = jax.ShapeDtypeStruct((5, 125, 256), F32)
+    operands = (
+        state, send_mem_idx, send_grp_idx, mem_count, grp_count, jnp.asarray(ext), coarse_nbr, face_src, rhs, fine_diag,
+        q_fine, var_mix, jnp.asarray(rest), jnp.asarray(rest_lift), owner.reshape(1, 256), coarse_diag.reshape(40, 256),
+        g_coarse.reshape(48, 8), q_coarse, jnp.asarray(small), jnp.asarray(lift),
+    )
     resid, second = pl.pallas_call(
         functools.partial(main_kernel, n_grp),
         out_shape=(field, jax.ShapeDtypeStruct((40, 256), F32)),
-        in_specs=[hbm] * 5 + [vmem, smem, smem, smem] + [vmem] * 11,
-        out_specs=(hbm, vmem),
-        scratch_shapes=[
-            pltpu.VMEM((5, 125, 256), F32),
-            pltpu.VMEM((5, 125, 256), F32),
-            pltpu.VMEM((5, 125, 256), F32),
-            pltpu.VMEM((768, 640), BF),
-            pltpu.VMEM((640, 768), BF),
+        in_specs=[hbm] * 20,
+        out_specs=(hbm, hbm),
+        scratch_shapes=[pltpu.VMEM(a.shape, a.dtype) for a in operands]
+        + [
             pltpu.VMEM((640, 256), BF),
             pltpu.VMEM((640, 256), BF),
             pltpu.VMEM((128, 128), F32),
@@ -350,28 +354,29 @@
             pltpu.VMEM((40, 256), F32),
             pltpu.VMEM((2, 80, 768), BF),
             pltpu.VMEM((5, 125, 256), F32),
-            pltpu.SemaphoreType.DMA((5,)),
+            pltpu.VMEM((40, 256), F32),
+            pltpu.SemaphoreType.DMA((20,)),
             pltpu.SemaphoreType.DMA((9,)),
             pltpu.SemaphoreType.DMA((10,)),
-            pltpu.SemaphoreType.DMA,
+            pltpu.SemaphoreType.DMA((2,)),
         ],
         compiler_params=pltpu.CompilerParams(
-            collective_id=0, has_side_effects=True, vmem_limit_bytes=40 * 1024 * 1024
+            collective_id=0, has_side_effects=True, vmem_limit_bytes=60 * 1024 * 1024
         ),
         name="residual_and_sweeps",
-    )(
-        state, rhs, fine_diag, jnp.asarray(ext), jnp.asarray(lift),
-        q_fine, var_mix, mem_count, grp_count, send_mem_idx, send_grp_idx, face_src,
-        coarse_diag.reshape(40, 256), q_coarse, g_coarse.reshape(48, 8), owner.reshape(1, 256), coarse_nbr,
-        jnp.asarray(rest), jnp.asarray(rest_lift), jnp.asarray(small),
-    )
+    )(*operands)
     return pl.pallas_call(
         last_kernel,
         out_shape=(field, field),
-        in_specs=[hbm, vmem, vmem],
+        in_specs=[hbm, hbm, hbm],
         out_specs=(hbm, hbm),
-        scratch_shapes=[pltpu.VMEM((5, 125, 256), F32), pltpu.SemaphoreType.DMA((6,))],
-        compiler_params=pltpu.CompilerParams(vmem_limit_bytes=16 * 1024 * 1024),
+        scratch_shapes=[
+            pltpu.VMEM((40, 256), F32),
+            pltpu.VMEM((640, 80), BF),
+            pltpu.VMEM((5, 125, 256), F32),
+            pltpu.SemaphoreType.DMA((8,)),
+        ],
+        compiler_params=pltpu.CompilerParams(vmem_limit_bytes=60 * 1024 * 1024),
         name="prolongation",
     )(resid, second, jnp.asarray(pro2))
 

time: 52.6 us -> 55 us (1.046); the launches traced: 51.8 us -> 54.9 us
  Pallas kernels: 35.7 us -> 54.2 us
  local copies, waits for them, and re-layouts: 15.4 us -> 0 us
    pallas_call x1, Pallas kernels: 1.1 us -> 21 us  [shards(): pl.pallas_call(last_kernel, out_shape=(field, field), in_specs=[hbm, hbm,...]
    unnamed x42 -> x0, local copies, waits for them, and re-layouts: 15.4 us -> none
    pallas_call x1, Pallas kernels: 34.6 us -> 33.2 us  [shards(): pl.pallas_call(functools.partial(main_kernel, n_grp), out_shape=(field, j...]
where the time goes in v2:
time: 55 us; the launch traced here: 54.9 us
  Pallas kernels  54.2 us (99%)
  between operations  0.64 us (1%)
    pallas_call x1, Pallas kernels, shards(): pl.pallas_call(functools.partial(main_kernel, n_grp), out_shape=(field, j...  33.2 us
    pallas_call x1, Pallas kernels, shards(): pl.pallas_call(last_kernel, out_shape=(field, field), in_specs=[hbm, hbm,...  21 us

profile of v2, /device:TPU:1, one launch (start us, length us, event | category | flops | bytes accessed | tf_op | source)
XLA Modules:
  0.0 54.9 jit_solution(2706444590164278326)
XLA Ops:
  0.6 33.2 %residual_and_sweeps.1 = (f32[5,125,256]{2,1,0:T(8,128)}, f32[40,256]{1,0:T(8,128)}) custom-call(f32[5,125,256]{2,1,0:T(8,128)} %refs_0_.1, s32[1,2,128]{2,1,0:T(2,128)} %refs_1_.1, s32[1,2,256]{2,1,0:T(2,128)} %refs_2_.1, s32[1,2]{1,0:T(1,128)} %refs_3_.1, s32[1,2]{1,0:T(1,128)} %refs_4_.1, bf16[768,640]{1,0:T(8,128)(2,1)} %constant.12.clone.refs_5_, ...), custom_call_target="tpu_custom_call" | custom-call | tf_op jit(solution)/shard_map/residual_and_sweeps/pallas_call | solution.py:329
  33.8 21.0 %prolongation.1 = (f32[5,125,256]{2,1,0:T(8,128)}, f32[5,125,256]{2,1,0:T(8,128)}) custom-call(f32[5,125,256]{2,1,0:T(8,128)} %get-tuple-element.4.resid, f32[40,256]{1,0:T(8,128)} %get-tuple-element.5.second_h, bf16[640,80]{1,0:T(8,128)(2,1)} %constant.17.clone.pro2_h), custom_call_target="tpu_custom_call" | custom-call | tf_op jit(solution)/shard_map/prolongation/pallas_call | solution.py:368

commit v3 on v2

--- a/solution.py
+++ b/solution.py
@@ -13,7 +13,6 @@
 HIGH = lax.Precision.HIGHEST
 BF = jnp.bfloat16
 F32 = jnp.float32
-FAR = 1 << 20
 
 
 def tables():
@@ -103,26 +102,55 @@
     (
         uh, ul, qs,
         ohs, tr, snd_g, snd_m, snd_n, rcv_g, rcv_m, rcv_n,
-        ohr, nlh, nll, resl, ohc, st_hot, blks, mine, rim, resv, mine2,
+        ohr, nlh, nll, resl, ohc, st_hot, blks, mine, rim, resv, mine2, near_acc,
         in_sem, snd_sem, rcv_sem, out_sem,
     ) = scratch[20:]
     g = lax.axis_index("grp")
     m = lax.axis_index("mem")
     other = 1 - m
-    prev = lax.rem(g + n_grp - 1, n_grp)
-    nxt = lax.rem(g + 1, n_grp)
+    has_prev, has_next = g > 0, g < n_grp - 1
+    prev, nxt = jnp.maximum(g - 1, 0), jnp.minimum(g + 1, n_grp - 1)
 
     loads = [pltpu.make_async_copy(src, scratch[i], in_sem.at[i]) for i, src in enumerate(sources)]
-    for c in loads:
+    for c in loads[:8]:
         c.start()
+    seen = set()
+
+    def need(*which):
+        for i in which:
+            if i not in seen:
+                seen.add(i)
+                loads[i].wait()
 
     barrier = pltpu.get_barrier_semaphore()
-    near_devices = [(prev, 0), (prev, 1), (nxt, 0), (nxt, 1), (g, other)]
-    for d in near_devices:
-        pl.semaphore_signal(barrier, inc=1, device_id=d, device_id_type=MESH)
-
-    for i in (1, 2, 3, 4, 6):
-        loads[i].wait()
+    def greet(device):
+        pl.semaphore_signal(barrier, inc=1, device_id=device, device_id_type=MESH)
+
+    greet((g, other))
+
+    @pl.when(has_prev)
+    def _():
+        greet((prev, 0))
+        greet((prev, 1))
+
+    @pl.when(has_next)
+    def _():
+        greet((nxt, 0))
+        greet((nxt, 1))
+
+    @pl.when(jnp.logical_not(has_prev))
+    def _():
+        rcv_g[0] = jnp.zeros((128, 256), F32)
+        blks[0] = jnp.zeros((40, 256), F32)
+        blks[1] = jnp.zeros((40, 256), F32)
+
+    @pl.when(jnp.logical_not(has_next))
+    def _():
+        rcv_g[1] = jnp.zeros((128, 256), F32)
+        blks[4] = jnp.zeros((40, 256), F32)
+        blks[5] = jnp.zeros((40, 256), F32)
+
+    need(1, 2, 3, 4, 6)
     lane_g = lax.broadcasted_iota(jnp.int32, (1, 256), 1)
     lane_m = lax.broadcasted_iota(jnp.int32, (1, 128), 1)
     for t in range(2):
@@ -135,12 +163,14 @@
     snd_n[0:6, :] = jnp.where(m == 0, nbr[:, 128:256], nbr[:, 0:128])
     snd_n[6:8, :] = jnp.zeros((2, 128), jnp.int32)
 
-    loads[0].wait()
+    need(0)
+    for c in loads[8:]:
+        c.start()
     for v in range(5):
         hi, lo = halves(padded(st[v]))
         uh[v * 128 : v * 128 + 128, :] = hi
         ul[v * 128 : v * 128 + 128, :] = lo
-    loads[5].wait()
+    need(5)
     for f in range(6):
         e = ext[f * 128 : f * 128 + 128, :]
         tr[0:128, f * 256 : f * 256 + 256] = dot(e, uh[...]).astype(BF)
@@ -152,24 +182,22 @@
             device_id=device, device_id_type=MESH,
         )
 
-    pl.semaphore_wait(barrier, 5)
+    pl.semaphore_wait(barrier, 1 + 2 * has_prev.astype(jnp.int32) + 2 * has_next.astype(jnp.int32))
     c_nbr = remote(snd_n, rcv_n, 0, 0, (g, other))
     c_nbr.start()
     picked = dot(tr[...], ohs[:, 0:256])
     snd_g[0] = picked[:128] + picked[128:]
     c_prev = remote(snd_g.at[0], rcv_g.at[1], 1, 1, (prev, m))
-    c_prev.start()
+    pl.when(has_prev)(c_prev.start)
     picked = dot(tr[...], ohs[:, 256:512])
     snd_g[1] = picked[:128] + picked[128:]
     c_next = remote(snd_g.at[1], rcv_g.at[0], 2, 2, (nxt, m))
-    c_next.start()
+    pl.when(has_next)(c_next.start)
     picked = dot(tr[...], ohs[:, 512:640])
     snd_m[...] = picked[:128] + picked[128:]
     c_mem = remote(snd_m, rcv_m, 3, 3, (g, other))
     c_mem.start()
 
-    base_prev = jnp.where(g == 0, FAR, 1792)
-    base_next = jnp.where(g == n_grp - 1, FAR, 2048)
     base_mem = 1536 + other * 128
 
     def local_faces(f, carry):
@@ -178,16 +206,15 @@
         at = pl.multiple_of(f * 128, 128)
         nlh[pl.ds(at, 128), :] = acc[:128].astype(BF)
         nll[pl.ds(at, 128), :] = acc[128:].astype(BF)
-        ohr[f, 0:256, :] = hot(row, base_prev, 256)
-        ohr[f, 256:512, :] = hot(row, base_next, 256)
+        ohr[f, 0:256, :] = hot(row, 1792, 256)
+        ohr[f, 256:512, :] = hot(row, 2048, 256)
         ohr[f, 512:640, :] = hot(row, base_mem, 128)
         return carry
 
-    loads[7].wait()
+    need(7)
     lax.fori_loop(0, 6, local_faces, 0)
 
-    for i in range(8, 19):
-        loads[i].wait()
+    need(*range(8, 19))
     qs[...] = jnp.zeros((128, 128), F32)
     qs[0:125, 0:125] = q_fine[...]
     qh, ql = halves(qs[...])
@@ -216,15 +243,19 @@
     qrep = jnp.concatenate([q_coarse[...]] * 5, axis=0)
     qq = exact(qrep, small[0:8, 0:40]) * small[104:144, 0:40]
 
-    c_prev.wait_recv()
-    c_next.wait_recv()
+    def both_halves(ref):
+        hi, lo = halves(ref[...])
+        return jnp.concatenate([hi, lo], axis=0)
+
     c_mem.wait_recv()
-    parts = []
-    for ref in (rcv_g.at[0], rcv_g.at[1], rcv_m):
-        hi, lo = halves(ref[...])
-        parts.append(jnp.concatenate([hi, lo], axis=0))
+    part = both_halves(rcv_m)
     for f in range(6):
-        acc = dot(parts[0], ohr[f, 0:256, :]) + dot(parts[1], ohr[f, 256:512, :]) + dot(parts[2], ohr[f, 512:640, :])
+        near_acc[f] = dot(part, ohr[f, 512:640, :])
+    pl.when(has_next)(c_prev.wait_recv)
+    pl.when(has_prev)(c_next.wait_recv)
+    parts = [both_halves(rcv_g.at[0]), both_halves(rcv_g.at[1])]
+    for f in range(6):
+        acc = near_acc[f] + dot(parts[0], ohr[f, 0:256, :]) + dot(parts[1], ohr[f, 256:512, :])
         nh, nl = acc[:128].astype(BF), acc[128:].astype(BF)
         rlf = rest_lift[:, f * 128 : f * 128 + 128]
         rest0 = rest0 + dot(rlf, nh) + dot(rlf, nl)
@@ -235,18 +266,25 @@
     packed = lax.dot_general(stacked(first), st_hot[...], (((1,), (1,)), ((), ())), preferred_element_type=F32)
     mine[...] = packed[:40] + packed[40:]
     c_two = []
-    for i, (d, place) in enumerate(
-        [((prev, 0), 4 + m), ((prev, 1), 4 + m), ((nxt, 0), m), ((nxt, 1), m), ((g, other), 2 + m)]
+    for i, (ok, d, place) in enumerate(
+        [
+            (has_prev, (prev, 0), 4 + m),
+            (has_prev, (prev, 1), 4 + m),
+            (has_next, (nxt, 0), m),
+            (has_next, (nxt, 1), m),
+            (None, (g, other), 2 + m),
+        ]
     ):
         c = remote(mine, blks.at[place], 4 + i, 4 + place, d)
-        c.start()
-        c_two.append(c)
-
+        c_two.append((ok, c))
+        if ok is None:
+            c.start()
+        else:
+            pl.when(ok)(c.start)
+
+    need(19)
     for v in range(5):
         lf = lift[v * 128 : v * 128 + 128, :]
-        if v == 0:
-            loads[19].wait()
-            lf = lift[0:128, :]
         full = resl[v * 128 : v * 128 + 128, :] + dot(lf, nlh[...]) + dot(lf, nll[...])
         resv[v] = full[:125]
     c_out = pltpu.make_async_copy(resv, resid_out, out_sem.at[0])
@@ -260,16 +298,24 @@
     got_nbr = rcv_n[0:6, :]
     for o in range(2):
         lists = jnp.where(m == o, own_nbr, got_nbr)
-        lists = jnp.where((g == 0) & (lists < 256), FAR, lists)
-        lists = jnp.where((g == n_grp - 1) & (lists >= 512), FAR, lists)
         for f in range(6):
             ohc[o, :, f * 128 : f * 128 + 128] = hot(lists[f : f + 1, :], 0, 768)
 
     def arrived(place):
         remote(mine, blks.at[place], 4, 4 + place, (g, other)).wait_recv()
 
-    for place in (2 + other, 0, 1, 4, 5):
-        arrived(place)
+    arrived(2 + other)
+
+    @pl.when(has_prev)
+    def _():
+        arrived(0)
+        arrived(1)
+
+    @pl.when(has_next)
+    def _():
+        arrived(4)
+        arrived(5)
+
     blks[2 + m] = mine[...]
     for j in range(6):
         both = stacked(blks[j])
@@ -288,25 +334,32 @@
     c_second = pltpu.make_async_copy(mine2, second_out, out_sem.at[1])
     c_second.start()
 
-    for c in [c_nbr, c_prev, c_next, c_mem] + c_two:
-        c.wait_send()
+    for ok, c in [(None, c_nbr), (has_prev, c_prev), (has_next, c_next), (None, c_mem)] + c_two:
+        if ok is None:
+            c.wait_send()
+        else:
+            pl.when(ok)(c.wait_send)
     c_out.wait()
     c_second.wait()
 
 
-def last_kernel(resid, second_h, pro2_h, resid_out, corr_out, second, pro2, corr, sem):
+def last_kernel(resid, second_h, pro2_h, resid_out, corr_out, second, pro2, corr, held, sem):
     loads = [pltpu.make_async_copy(second_h, second, sem.at[0]), pltpu.make_async_copy(pro2_h, pro2, sem.at[1])]
-    whole = pltpu.make_async_copy(resid, resid_out, sem.at[2])
+    loads += [pltpu.make_async_copy(resid.at[v], held.at[v], sem.at[2 + v]) for v in range(5)]
     for c in loads:
         c.start()
-    whole.start()
-    for c in loads:
-        c.wait()
+    copies = []
+    for v in range(5):
+        loads[2 + v].wait()
+        c = pltpu.make_async_copy(held.at[v], resid_out.at[v], sem.at[7 + v])
+        c.start()
+        copies.append(c)
+    loads[0].wait()
+    loads[1].wait()
     both = stacked(second[...])
-    copies = [whole]
     for v in range(5):
         corr[v] = dot(pro2[v * 128 : v * 128 + 128, :], both)[:125]
-        c = pltpu.make_async_copy(corr.at[v], corr_out.at[v], sem.at[3 + v])
+        c = pltpu.make_async_copy(corr.at[v], corr_out.at[v], sem.at[12 + v])
         c.start()
         copies.append(c)
     for c in copies:
@@ -355,6 +408,7 @@
             pltpu.VMEM((2, 80, 768), BF),
             pltpu.VMEM((5, 125, 256), F32),
             pltpu.VMEM((40, 256), F32),
+            pltpu.VMEM((6, 256, 256), F32),
             pltpu.SemaphoreType.DMA((20,)),
             pltpu.SemaphoreType.DMA((9,)),
             pltpu.SemaphoreType.DMA((10,)),
@@ -374,7 +428,8 @@
             pltpu.VMEM((40, 256), F32),
             pltpu.VMEM((640, 80), BF),
             pltpu.VMEM((5, 125, 256), F32),
-            pltpu.SemaphoreType.DMA((8,)),
+            pltpu.VMEM((5, 125, 256), F32),
+            pltpu.SemaphoreType.DMA((17,)),
         ],
         compiler_params=pltpu.CompilerParams(vmem_limit_bytes=60 * 1024 * 1024),
         name="prolongation",

time: 55 us -> 26.2 us (0.48)
  the two profiles are of different devices: /device:TPU:1 before, /device:TPU:257 now
where the time goes in v3:
time: 26.2 us; the launch traced here: 26.1 us
  Pallas kernels  25.4 us (97%)
  between operations  0.64 us (2%)
    pallas_call x1, Pallas kernels, shards(): pl.pallas_call(functools.partial(main_kernel, n_grp), out_shape=(field, j...  23.1 us
    pallas_call x1, Pallas kernels, shards(): pl.pallas_call(last_kernel, out_shape=(field, field), in_specs=[hbm, hbm,...  2.36 us

profile of v3, /device:TPU:257, one launch (start us, length us, event | category | flops | bytes accessed | tf_op | source)
XLA Modules:
  0.0 26.1 jit_solution(12175268325682246252)
XLA Ops:
  0.6 23.1 %residual_and_sweeps.1 = (f32[5,125,256]{2,1,0:T(8,128)}, f32[40,256]{1,0:T(8,128)}) custom-call(f32[5,125,256]{2,1,0:T(8,128)} %refs_0_.1, s32[1,2,128]{2,1,0:T(2,128)} %refs_1_.1, s32[1,2,256]{2,1,0:T(2,128)} %refs_2_.1, s32[1,2]{1,0:T(1,128)} %refs_3_.1, s32[1,2]{1,0:T(1,128)} %refs_4_.1, bf16[768,640]{1,0:T(8,128)(2,1)} %constant.12.clone.refs_5_, ...), custom_call_target="tpu_custom_call" | custom-call | tf_op jit(solution)/shard_map/residual_and_sweeps/pallas_call | solution.py:382
  23.7 2.4 %prolongation.1 = (f32[5,125,256]{2,1,0:T(8,128)}, f32[5,125,256]{2,1,0:T(8,128)}) custom-call(f32[5,125,256]{2,1,0:T(8,128)} %get-tuple-element.4.resid, f32[40,256]{1,0:T(8,128)} %get-tuple-element.5.second_h, bf16[640,80]{1,0:T(8,128)(2,1)} %constant.17.clone.pro2_h), custom_call_target="tpu_custom_call" | custom-call | tf_op jit(solution)/shard_map/prolongation/pallas_call | solution.py:422

commit v4 on v3

--- a/solution.py
+++ b/solution.py
@@ -32,12 +32,18 @@
     for v in range(5):
         ext[:, v * 25 : v * 25 + 25, v, :125] = extract
     ext = ext.reshape(768, 640)
+    places = np.full((8, 640), -1, np.int32)
+    for face in range(6):
+        block = ext[face * 128 : face * 128 + 128]
+        places[face] = np.where(block.any(axis=0), block.argmax(axis=0), -1)
     lift = np.ascontiguousarray(ext.T)
     rest = np.zeros((48, 5, 128), np.float32)
     for v in range(5):
         rest[v * 8 : v * 8 + 8, v, :125] = prolong.T
     rest = rest.reshape(48, 640)
     rest_lift = rest @ lift
+    by_face = rest_lift.reshape(48, 6, 128).transpose(1, 0, 2).reshape(288, 128)
+    by_face = np.concatenate([by_face, by_face], axis=1)
     pro = np.ascontiguousarray(rest[:40].T)
     pro2 = np.concatenate([pro, pro], axis=1)
     spread = np.zeros((8, 6, 5, 8), np.float32)
@@ -63,7 +69,7 @@
     small[56:104] = same_f
     small[104:152] = same_v
     cast = lambda a: np.asarray(a, ml_dtypes.bfloat16)
-    return cast(ext), cast(lift), cast(rest), cast(rest_lift), cast(pro2), small
+    return places, cast(lift), cast(rest), cast(rest_lift), cast(by_face), cast(pro2), small
 
 
 def halves(x):
@@ -85,8 +91,9 @@
 
 
 def hot(row, base, size):
-    places = lax.broadcasted_iota(jnp.int32, (size, row.shape[1]), 0)
-    return jnp.where(places == row - base, 1.0, 0.0).astype(BF)
+    row = (row - base).astype(jnp.int16)
+    places = lax.broadcasted_iota(jnp.int16, (size, row.shape[1]), 0)
+    return jnp.where(places == row, jnp.ones((), BF), jnp.zeros((), BF))
 
 
 def padded(x):
@@ -94,17 +101,17 @@
 
 
 def main_kernel(n_grp, *refs):
-    sources, (resid_out, second_out), scratch = refs[:20], refs[20:22], refs[22:]
+    sources, (resid_out, second_out), scratch = refs[:21], refs[21:23], refs[23:]
     (
-        st, midx, gidx, mcount, gcount, ext, cnbr, fsrc, rh, dg, q_fine, var_mix,
-        rest, rest_lift, owner, cdiag, g_coarse, q_coarse, small, lift,
-    ) = scratch[:20]
+        st, midx, gidx, mcount, gcount, places, cnbr, fsrc, rh, dg, q_fine, var_mix,
+        rest, rest_lift, owner, cdiag, g_coarse, q_coarse, small, by_face, lift,
+    ) = scratch[:21]
     (
         uh, ul, qs,
         ohs, tr, snd_g, snd_m, snd_n, rcv_g, rcv_m, rcv_n,
-        ohr, nlh, nll, resl, ohc, st_hot, blks, mine, rim, resv, mine2, near_acc,
+        ohr, nlh, nll, resl, ohc, st_hot, blks, mine, rim, resv, mine2, ext, arrived_hl, zs,
         in_sem, snd_sem, rcv_sem, out_sem,
-    ) = scratch[20:]
+    ) = scratch[21:]
     g = lax.axis_index("grp")
     m = lax.axis_index("mem")
     other = 1 - m
@@ -150,7 +157,7 @@
         blks[4] = jnp.zeros((40, 256), F32)
         blks[5] = jnp.zeros((40, 256), F32)
 
-    need(1, 2, 3, 4, 6)
+    need(1, 2, 3, 4, 5, 6)
     lane_g = lax.broadcasted_iota(jnp.int32, (1, 256), 1)
     lane_m = lax.broadcasted_iota(jnp.int32, (1, 128), 1)
     for t in range(2):
@@ -163,6 +170,9 @@
     snd_n[0:6, :] = jnp.where(m == 0, nbr[:, 128:256], nbr[:, 0:128])
     snd_n[6:8, :] = jnp.zeros((2, 128), jnp.int32)
 
+    for f in range(6):
+        ext[f * 128 : f * 128 + 128, :] = hot(places[f : f + 1, :], 0, 128)
+
     need(0)
     for c in loads[8:]:
         c.start()
@@ -170,7 +180,6 @@
         hi, lo = halves(padded(st[v]))
         uh[v * 128 : v * 128 + 128, :] = hi
         ul[v * 128 : v * 128 + 128, :] = lo
-    need(5)
     for f in range(6):
         e = ext[f * 128 : f * 128 + 128, :]
         tr[0:128, f * 256 : f * 256 + 256] = dot(e, uh[...]).astype(BF)
@@ -214,7 +223,7 @@
     need(7)
     lax.fori_loop(0, 6, local_faces, 0)
 
-    need(*range(8, 19))
+    need(*range(8, 20))
     qs[...] = jnp.zeros((128, 128), F32)
     qs[0:125, 0:125] = q_fine[...]
     qh, ql = halves(qs[...])
@@ -228,6 +237,7 @@
     rl_h, rl_l = halves(resl[...])
     rest0 = dot(rest[...], rl_h) + dot(rest[...], rl_l)
     rest0 = rest0 + dot(rest_lift[...], nlh[...]) + dot(rest_lift[...], nll[...])
+    rest0 = rest0[:40]
 
     own = owner[...].astype(F32)
     before = lax.broadcasted_iota(jnp.int32, (256, 256), 0) < lax.broadcasted_iota(jnp.int32, (256, 256), 1)
@@ -243,26 +253,31 @@
     qrep = jnp.concatenate([q_coarse[...]] * 5, axis=0)
     qq = exact(qrep, small[0:8, 0:40]) * small[104:144, 0:40]
 
-    def both_halves(ref):
+    c_nbr.wait_recv()
+    own_nbr = jnp.where(m == 0, nbr[:, 0:128], nbr[:, 128:256])
+    got_nbr = rcv_n[0:6, :]
+    for o in range(2):
+        lists = jnp.where(m == o, own_nbr, got_nbr)
+        for f in range(6):
+            ohc[o, :, f * 128 : f * 128 + 128] = hot(lists[f : f + 1, :], 0, 768)
+
+    def take(ref, at, width):
         hi, lo = halves(ref[...])
-        return jnp.concatenate([hi, lo], axis=0)
+        arrived_hl[0:128, at : at + width] = hi
+        arrived_hl[128:256, at : at + width] = lo
 
     c_mem.wait_recv()
-    part = both_halves(rcv_m)
-    for f in range(6):
-        near_acc[f] = dot(part, ohr[f, 512:640, :])
+    take(rcv_m, 512, 128)
     pl.when(has_next)(c_prev.wait_recv)
     pl.when(has_prev)(c_next.wait_recv)
-    parts = [both_halves(rcv_g.at[0]), both_halves(rcv_g.at[1])]
+    take(rcv_g.at[0], 0, 256)
+    take(rcv_g.at[1], 256, 256)
+    zs[...] = dot(by_face[...], arrived_hl[...])
     for f in range(6):
-        acc = near_acc[f] + dot(parts[0], ohr[f, 0:256, :]) + dot(parts[1], ohr[f, 256:512, :])
-        nh, nl = acc[:128].astype(BF), acc[128:].astype(BF)
-        rlf = rest_lift[:, f * 128 : f * 128 + 128]
-        rest0 = rest0 + dot(rlf, nh) + dot(rlf, nl)
-        nlh[f * 128 : f * 128 + 128, :] += nh
-        nll[f * 128 : f * 128 + 128, :] += nl
+        part = dot(stacked(zs[f * 48 : f * 48 + 40, :]), ohr[f])
+        rest0 = rest0 + (part[:40] + part[40:])
     cd = cdiag[...]
-    first = (0.8 * 0.064) * rest0[:40] / cd
+    first = (0.8 * 0.064) * rest0 / cd
     packed = lax.dot_general(stacked(first), st_hot[...], (((1,), (1,)), ((), ())), preferred_element_type=F32)
     mine[...] = packed[:40] + packed[40:]
     c_two = []
@@ -282,7 +297,11 @@
         else:
             pl.when(ok)(c.start)
 
-    need(19)
+    for f in range(6):
+        acc = dot(arrived_hl[...], ohr[f])
+        nlh[f * 128 : f * 128 + 128, :] += acc[:128].astype(BF)
+        nll[f * 128 : f * 128 + 128, :] += acc[128:].astype(BF)
+    need(20)
     for v in range(5):
         lf = lift[v * 128 : v * 128 + 128, :]
         full = resl[v * 128 : v * 128 + 128, :] + dot(lf, nlh[...]) + dot(lf, nll[...])
@@ -292,14 +311,6 @@
     inner = exact(qq, first)
     weight = 0.8 / cd
     base = 1.2 * first - weight * inner
-
-    c_nbr.wait_recv()
-    own_nbr = jnp.where(m == 0, nbr[:, 0:128], nbr[:, 128:256])
-    got_nbr = rcv_n[0:6, :]
-    for o in range(2):
-        lists = jnp.where(m == o, own_nbr, got_nbr)
-        for f in range(6):
-            ohc[o, :, f * 128 : f * 128 + 128] = hot(lists[f : f + 1, :], 0, 768)
 
     def arrived(place):
         remote(mine, blks.at[place], 4, 4 + place, (g, other)).wait_recv()
@@ -370,19 +381,19 @@
     state, rhs, fine_diag, q_fine, var_mix, mem_count, grp_count, send_mem_idx, send_grp_idx,
     face_src, coarse_diag, q_coarse, g_coarse, owner, coarse_nbr,
 ):
-    ext, lift, rest, rest_lift, pro2, small = tables()
+    places, lift, rest, rest_lift, by_face, pro2, small = tables()
     n_grp = lax.axis_size("grp")
     hbm = pl.BlockSpec(memory_space=pltpu.HBM)
     field = jax.ShapeDtypeStruct((5, 125, 256), F32)
     operands = (
-        state, send_mem_idx, send_grp_idx, mem_count, grp_count, jnp.asarray(ext), coarse_nbr, face_src, rhs, fine_diag,
+        state, send_mem_idx, send_grp_idx, mem_count, grp_count, jnp.asarray(places), coarse_nbr, face_src, rhs, fine_diag,
         q_fine, var_mix, jnp.asarray(rest), jnp.asarray(rest_lift), owner.reshape(1, 256), coarse_diag.reshape(40, 256),
-        g_coarse.reshape(48, 8), q_coarse, jnp.asarray(small), jnp.asarray(lift),
+        g_coarse.reshape(48, 8), q_coarse, jnp.asarray(small), jnp.asarray(by_face), jnp.asarray(lift),
     )
     resid, second = pl.pallas_call(
         functools.partial(main_kernel, n_grp),
         out_shape=(field, jax.ShapeDtypeStruct((40, 256), F32)),
-        in_specs=[hbm] * 20,
+        in_specs=[hbm] * 21,
         out_specs=(hbm, hbm),
         scratch_shapes=[pltpu.VMEM(a.shape, a.dtype) for a in operands]
         + [
@@ -408,8 +419,10 @@
             pltpu.VMEM((2, 80, 768), BF),
             pltpu.VMEM((5, 125, 256), F32),
             pltpu.VMEM((40, 256), F32),
-            pltpu.VMEM((6, 256, 256), F32),
-            pltpu.SemaphoreType.DMA((20,)),
+            pltpu.VMEM((768, 640), BF),
+            pltpu.VMEM((256, 640), BF),
+            pltpu.VMEM((288, 640), F32),
+            pltpu.SemaphoreType.DMA((21,)),
             pltpu.SemaphoreType.DMA((9,)),
             pltpu.SemaphoreType.DMA((10,)),
             pltpu.SemaphoreType.DMA((2,)),

time: 26.2 us -> 25.5 us (0.973)
  Pallas kernels: 25.4 us -> 24.7 us
    pallas_call x1, Pallas kernels: 23.1 us -> 22.3 us  [shards(): pl.pallas_call(functools.partial(main_kernel, n_grp), out_shape=(field, j...]
where the time goes in v4:
time: 25.5 us; the launch traced here: 25.3 us
  Pallas kernels  24.7 us (97%)
  between operations  0.64 us (3%)
    pallas_call x1, Pallas kernels, shards(): pl.pallas_call(functools.partial(main_kernel, n_grp), out_shape=(field, j...  22.3 us
    pallas_call x1, Pallas kernels, shards(): pl.pallas_call(last_kernel, out_shape=(field, field), in_specs=[hbm, hbm,...  2.37 us

profile of v4, /device:TPU:257, one launch (start us, length us, event | category | flops | bytes accessed | tf_op | source)
XLA Modules:
  0.0 25.3 jit_solution(7961907311902374868)
XLA Ops:
  0.6 22.3 %residual_and_sweeps.1 = (f32[5,125,256]{2,1,0:T(8,128)}, f32[40,256]{1,0:T(8,128)}) custom-call(f32[5,125,256]{2,1,0:T(8,128)} %refs_0_.1, s32[1,2,128]{2,1,0:T(2,128)} %refs_1_.1, s32[1,2,256]{2,1,0:T(2,128)} %refs_2_.1, s32[1,2]{1,0:T(1,128)} %refs_3_.1, s32[1,2]{1,0:T(1,128)} %refs_4_.1, s32[8,640]{1,0:T(8,128)} %constant.14.clone.refs_5_, ...), custom_call_target="tpu_custom_call" | custom-call | tf_op jit(solution)/shard_map/residual_and_sweeps/pallas_call | solution.py:393
  22.9 2.4 %prolongation.1 = (f32[5,125,256]{2,1,0:T(8,128)}, f32[5,125,256]{2,1,0:T(8,128)}) custom-call(f32[5,125,256]{2,1,0:T(8,128)} %get-tuple-element.4.resid, f32[40,256]{1,0:T(8,128)} %get-tuple-element.5.second_h, bf16[640,80]{1,0:T(8,128)(2,1)} %constant.20.clone.pro2_h), custom_call_target="tpu_custom_call" | custom-call | tf_op jit(solution)/shard_map/prolongation/pallas_call | solution.py:435

commit v5 on v4

--- a/solution.py
+++ b/solution.py
@@ -44,8 +44,7 @@
     rest_lift = rest @ lift
     by_face = rest_lift.reshape(48, 6, 128).transpose(1, 0, 2).reshape(288, 128)
     by_face = np.concatenate([by_face, by_face], axis=1)
-    pro = np.ascontiguousarray(rest[:40].T)
-    pro2 = np.concatenate([pro, pro], axis=1)
+    pro2 = np.concatenate([rest[:8, :128].T, rest[:8, :128].T], axis=1)
     spread = np.zeros((8, 6, 5, 8), np.float32)
     for b in range(8):
         spread[b, :, :, b] = 1.0
@@ -108,18 +107,20 @@
     ) = scratch[:21]
     (
         uh, ul, qs,
-        ohs, tr, snd_g, snd_m, snd_n, rcv_g, rcv_m, rcv_n,
-        ohr, nlh, nll, resl, ohc, st_hot, blks, mine, rim, resv, mine2, ext, arrived_hl, zs,
-        in_sem, snd_sem, rcv_sem, out_sem,
+        ohs, ohm, tr, snd_g, snd_m, snd_n, rcv_g, rcv_m, rcv_n,
+        ohr, ohrm, nlh, nll, resl, ohc, st_hot, blks, mine, resv, mine2, ext, arr_g, arr_m,
+        in_sem, st_sem, snd_sem, rcv_sem, out_sem,
     ) = scratch[21:]
     g = lax.axis_index("grp")
     m = lax.axis_index("mem")
     other = 1 - m
     has_prev, has_next = g > 0, g < n_grp - 1
+    far = jnp.where(lax.rem(g, 4) == 3, 1, 0)
     prev, nxt = jnp.maximum(g - 1, 0), jnp.minimum(g + 1, n_grp - 1)
 
-    loads = [pltpu.make_async_copy(src, scratch[i], in_sem.at[i]) for i, src in enumerate(sources)]
-    for c in loads[:8]:
+    loads = [None] + [pltpu.make_async_copy(sources[i], scratch[i], in_sem.at[i]) for i in range(1, 21)]
+    fields = [pltpu.make_async_copy(sources[0].at[v], st.at[v], st_sem.at[v]) for v in range(5)]
+    for c in loads[1:7] + fields + loads[7:8]:
         c.start()
     seen = set()
 
@@ -162,10 +163,10 @@
     lane_m = lax.broadcasted_iota(jnp.int32, (1, 128), 1)
     for t in range(2):
         row = jnp.where(lane_g < gcount[0:1, t : t + 1], gidx[0, t : t + 1, :], -1)
-        ohs[:, t * 256 : t * 256 + 256] = hot(row, 0, 1536)
+        ohs[t] = hot(row, 0, 1536)
     mrow = jnp.where(m == 0, midx[0, 1:2, :], midx[0, 0:1, :])
     mlim = jnp.where(m == 0, mcount[0:1, 1:2], mcount[0:1, 0:1])
-    ohs[:, 512:640] = hot(jnp.where(lane_m < mlim, mrow, -1), 0, 1536)
+    ohm[...] = hot(jnp.where(lane_m < mlim, mrow, -1), 0, 1536)
     nbr = cnbr[...]
     snd_n[0:6, :] = jnp.where(m == 0, nbr[:, 128:256], nbr[:, 0:128])
     snd_n[6:8, :] = jnp.zeros((2, 128), jnp.int32)
@@ -173,10 +174,10 @@
     for f in range(6):
         ext[f * 128 : f * 128 + 128, :] = hot(places[f : f + 1, :], 0, 128)
 
-    need(0)
     for c in loads[8:]:
         c.start()
     for v in range(5):
+        fields[v].wait()
         hi, lo = halves(padded(st[v]))
         uh[v * 128 : v * 128 + 128, :] = hi
         ul[v * 128 : v * 128 + 128, :] = lo
@@ -194,15 +195,18 @@
     pl.semaphore_wait(barrier, 1 + 2 * has_prev.astype(jnp.int32) + 2 * has_next.astype(jnp.int32))
     c_nbr = remote(snd_n, rcv_n, 0, 0, (g, other))
     c_nbr.start()
-    picked = dot(tr[...], ohs[:, 0:256])
-    snd_g[0] = picked[:128] + picked[128:]
-    c_prev = remote(snd_g.at[0], rcv_g.at[1], 1, 1, (prev, m))
-    pl.when(has_prev)(c_prev.start)
-    picked = dot(tr[...], ohs[:, 256:512])
-    snd_g[1] = picked[:128] + picked[128:]
-    c_next = remote(snd_g.at[1], rcv_g.at[0], 2, 2, (nxt, m))
-    pl.when(has_next)(c_next.start)
-    picked = dot(tr[...], ohs[:, 512:640])
+    def side(t):
+        return jnp.where(t == 0, prev, nxt), jnp.where(t == 0, has_prev, has_next)
+
+    c_grp = []
+    for t in (far, 1 - far):
+        group, there = side(t)
+        picked = dot(tr[...], ohs[t])
+        snd_g[t] = picked[:128] + picked[128:]
+        c = remote(snd_g.at[t], rcv_g.at[1 - t], 1 + t, 2 - t, (group, m))
+        pl.when(there)(c.start)
+        c_grp.append((there, c))
+    picked = dot(tr[...], ohm[...])
     snd_m[...] = picked[:128] + picked[128:]
     c_mem = remote(snd_m, rcv_m, 3, 3, (g, other))
     c_mem.start()
@@ -215,9 +219,9 @@
         at = pl.multiple_of(f * 128, 128)
         nlh[pl.ds(at, 128), :] = acc[:128].astype(BF)
         nll[pl.ds(at, 128), :] = acc[128:].astype(BF)
-        ohr[f, 0:256, :] = hot(row, 1792, 256)
-        ohr[f, 256:512, :] = hot(row, 2048, 256)
-        ohr[f, 512:640, :] = hot(row, base_mem, 128)
+        ohr[0, f] = hot(row, 1792, 256)
+        ohr[1, f] = hot(row, 2048, 256)
+        ohrm[f] = hot(row, base_mem, 128)
         return carry
 
     need(7)
@@ -259,46 +263,44 @@
     for o in range(2):
         lists = jnp.where(m == o, own_nbr, got_nbr)
         for f in range(6):
-            ohc[o, :, f * 128 : f * 128 + 128] = hot(lists[f : f + 1, :], 0, 768)
-
-    def take(ref, at, width):
+            for d in range(3):
+                ohc[o, d, :, f * 128 : f * 128 + 128] = hot(lists[f : f + 1, :], d * 256, 256)
+
+    def take(ref):
         hi, lo = halves(ref[...])
-        arrived_hl[0:128, at : at + width] = hi
-        arrived_hl[128:256, at : at + width] = lo
+        return jnp.concatenate([hi, lo], axis=0)
 
     c_mem.wait_recv()
-    take(rcv_m, 512, 128)
-    pl.when(has_next)(c_prev.wait_recv)
-    pl.when(has_prev)(c_next.wait_recv)
-    take(rcv_g.at[0], 0, 256)
-    take(rcv_g.at[1], 256, 256)
-    zs[...] = dot(by_face[...], arrived_hl[...])
+    arr_m[...] = take(rcv_m)
+    z = dot(by_face[...], arr_m[...])
     for f in range(6):
-        part = dot(stacked(zs[f * 48 : f * 48 + 40, :]), ohr[f])
+        part = dot(stacked(z[f * 48 : f * 48 + 40]), ohrm[f])
         rest0 = rest0 + (part[:40] + part[40:])
+    for t in (1 - far, far):
+        group, there = side(t)
+        pl.when(there)(remote(snd_g.at[t], rcv_g.at[t], 1 + t, 1 + t, (group, m)).wait_recv)
+        arr_g[t] = take(rcv_g.at[t])
+        z = dot(by_face[...], arr_g[t])
+        for f in range(6):
+            part = dot(stacked(z[f * 48 : f * 48 + 40]), ohr[t, f])
+            rest0 = rest0 + (part[:40] + part[40:])
     cd = cdiag[...]
     first = (0.8 * 0.064) * rest0 / cd
     packed = lax.dot_general(stacked(first), st_hot[...], (((1,), (1,)), ((), ())), preferred_element_type=F32)
     mine[...] = packed[:40] + packed[40:]
     c_two = []
-    for i, (ok, d, place) in enumerate(
-        [
-            (has_prev, (prev, 0), 4 + m),
-            (has_prev, (prev, 1), 4 + m),
-            (has_next, (nxt, 0), m),
-            (has_next, (nxt, 1), m),
-            (None, (g, other), 2 + m),
-        ]
-    ):
-        c = remote(mine, blks.at[place], 4 + i, 4 + place, d)
-        c_two.append((ok, c))
-        if ok is None:
-            c.start()
-        else:
-            pl.when(ok)(c.start)
+    for t in (far, 1 - far):
+        group, there = side(t)
+        place = jnp.where(t == 0, 4 + m, m)
+        for k in range(2):
+            c = remote(mine, blks.at[place], 4 + 2 * t + k, 4 + place, (group, k))
+            pl.when(there)(c.start)
+            c_two.append((there, c))
+    c_own = remote(mine, blks.at[2 + m], 8, 6 + m, (g, other))
+    c_own.start()
 
     for f in range(6):
-        acc = dot(arrived_hl[...], ohr[f])
+        acc = dot(arr_g[0], ohr[0, f]) + dot(arr_g[1], ohr[1, f]) + dot(arr_m[...], ohrm[f])
         nlh[f * 128 : f * 128 + 128, :] += acc[:128].astype(BF)
         nll[f * 128 : f * 128 + 128, :] += acc[128:].astype(BF)
     need(20)
@@ -313,28 +315,29 @@
     base = 1.2 * first - weight * inner
 
     def arrived(place):
-        remote(mine, blks.at[place], 4, 4 + place, (g, other)).wait_recv()
+        remote(mine, blks.at[place], 8, 4 + place, (g, other)).wait_recv()
+
+    def neighbours(d):
+        a, b = stacked(blks[2 * d]), stacked(blks[2 * d + 1])
+        return [
+            dot(jnp.concatenate([a[:, o * 128 : o * 128 + 128], b[:, o * 128 : o * 128 + 128]], axis=1), ohc[o, d])
+            for o in range(2)
+        ]
 
     arrived(2 + other)
-
-    @pl.when(has_prev)
-    def _():
-        arrived(0)
-        arrived(1)
-
-    @pl.when(has_next)
-    def _():
-        arrived(4)
-        arrived(5)
-
     blks[2 + m] = mine[...]
-    for j in range(6):
-        both = stacked(blks[j])
-        rim[0, :, j * 128 : j * 128 + 128] = both[:, 0:128]
-        rim[1, :, j * 128 : j * 128 + 128] = both[:, 128:256]
+    nears = neighbours(1)
+    for t in (1 - far, far):
+
+        @pl.when(side(t)[1])
+        def _(t=t):
+            arrived(4 * t)
+            arrived(4 * t + 1)
+
+        nears = [x + y for x, y in zip(nears, neighbours(2 * t))]
     nhs, nls = [], []
     for o in range(2):
-        near = dot(rim[o], ohc[o])
+        near = nears[o]
         nhs.append(jnp.concatenate([near[:40, f * 128 : f * 128 + 128] for f in range(6)], axis=0))
         nls.append(jnp.concatenate([near[40:, f * 128 : f * 128 + 128] for f in range(6)], axis=0))
     nh = jnp.concatenate(nhs, axis=1).astype(BF)
@@ -345,11 +348,10 @@
     c_second = pltpu.make_async_copy(mine2, second_out, out_sem.at[1])
     c_second.start()
 
-    for ok, c in [(None, c_nbr), (has_prev, c_prev), (has_next, c_next), (None, c_mem)] + c_two:
-        if ok is None:
-            c.wait_send()
-        else:
-            pl.when(ok)(c.wait_send)
+    for c in (c_nbr, c_mem, c_own):
+        c.wait_send()
+    for there, c in c_grp + c_two:
+        pl.when(there)(c.wait_send)
     c_out.wait()
     c_second.wait()
 
@@ -360,16 +362,14 @@
     for c in loads:
         c.start()
     copies = []
-    for v in range(5):
+    loads[0].wait()
+    loads[1].wait()
+    for v in range(5):
+        corr[v] = dot(pro2[...], stacked(second[v * 8 : v * 8 + 8, :]))[:125]
         loads[2 + v].wait()
         c = pltpu.make_async_copy(held.at[v], resid_out.at[v], sem.at[7 + v])
         c.start()
         copies.append(c)
-    loads[0].wait()
-    loads[1].wait()
-    both = stacked(second[...])
-    for v in range(5):
-        corr[v] = dot(pro2[v * 128 : v * 128 + 128, :], both)[:125]
         c = pltpu.make_async_copy(corr.at[v], corr_out.at[v], sem.at[12 + v])
         c.start()
         copies.append(c)
@@ -400,7 +400,8 @@
             pltpu.VMEM((640, 256), BF),
             pltpu.VMEM((640, 256), BF),
             pltpu.VMEM((128, 128), F32),
-            pltpu.VMEM((1536, 640), BF),
+            pltpu.VMEM((2, 1536, 256), BF),
+            pltpu.VMEM((1536, 128), BF),
             pltpu.VMEM((256, 1536), BF),
             pltpu.VMEM((2, 128, 256), F32),
             pltpu.VMEM((128, 128), F32),
@@ -408,21 +409,22 @@
             pltpu.VMEM((2, 128, 256), F32),
             pltpu.VMEM((128, 128), F32),
             pltpu.VMEM((8, 128), jnp.int32),
-            pltpu.VMEM((6, 640, 256), BF),
+            pltpu.VMEM((2, 6, 256, 256), BF),
+            pltpu.VMEM((6, 128, 256), BF),
             pltpu.VMEM((768, 256), BF),
             pltpu.VMEM((768, 256), BF),
             pltpu.VMEM((640, 256), F32),
-            pltpu.VMEM((2, 768, 768), BF),
+            pltpu.VMEM((2, 3, 256, 768), BF),
             pltpu.VMEM((256, 256), BF),
             pltpu.VMEM((6, 40, 256), F32),
             pltpu.VMEM((40, 256), F32),
-            pltpu.VMEM((2, 80, 768), BF),
             pltpu.VMEM((5, 125, 256), F32),
             pltpu.VMEM((40, 256), F32),
             pltpu.VMEM((768, 640), BF),
-            pltpu.VMEM((256, 640), BF),
-            pltpu.VMEM((288, 640), F32),
+            pltpu.VMEM((2, 256, 256), BF),
+            pltpu.VMEM((256, 128), BF),
             pltpu.SemaphoreType.DMA((21,)),
+            pltpu.SemaphoreType.DMA((5,)),
             pltpu.SemaphoreType.DMA((9,)),
             pltpu.SemaphoreType.DMA((10,)),
             pltpu.SemaphoreType.DMA((2,)),
@@ -439,7 +441,7 @@
         out_specs=(hbm, hbm),
         scratch_shapes=[
             pltpu.VMEM((40, 256), F32),
-            pltpu.VMEM((640, 80), BF),
+            pltpu.VMEM((128, 16), BF),
             pltpu.VMEM((5, 125, 256), F32),
             pltpu.VMEM((5, 125, 256), F32),
             pltpu.SemaphoreType.DMA((17,)),

time: 25.5 us -> 25.1 us (0.984)
  Pallas kernels: 24.7 us -> 24.3 us
    pallas_call x1, Pallas kernels: 22.3 us -> 21.9 us  [shards(): pl.pallas_call(functools.partial(main_kernel, n_grp), out_shape=(field, j...]
where the time goes in v5:
time: 25.1 us; the launch traced here: 25 us
  Pallas kernels  24.3 us (97%)
  between operations  0.64 us (3%)
    pallas_call x1, Pallas kernels, shards(): pl.pallas_call(functools.partial(main_kernel, n_grp), out_shape=(field, j...  21.9 us
    pallas_call x1, Pallas kernels, shards(): pl.pallas_call(last_kernel, out_shape=(field, field), in_specs=[hbm, hbm,...  2.42 us

profile of v5, /device:TPU:257, one launch (start us, length us, event | category | flops | bytes accessed | tf_op | source)
XLA Modules:
  0.0 25.0 jit_solution(13368254702213755966)
XLA Ops:
  0.6 21.9 %residual_and_sweeps.1 = (f32[5,125,256]{2,1,0:T(8,128)}, f32[40,256]{1,0:T(8,128)}) custom-call(f32[5,125,256]{2,1,0:T(8,128)} %refs_0_.1, s32[1,2,128]{2,1,0:T(2,128)} %refs_1_.1, s32[1,2,256]{2,1,0:T(2,128)} %refs_2_.1, s32[1,2]{1,0:T(1,128)} %refs_3_.1, s32[1,2]{1,0:T(1,128)} %refs_4_.1, s32[8,640]{1,0:T(8,128)} %constant.14.clone.refs_5_, ...), custom_call_target="tpu_custom_call" | custom-call | tf_op jit(solution)/shard_map/residual_and_sweeps/pallas_call | solution.py:393
  22.5 2.4 %prolongation.1 = (f32[5,125,256]{2,1,0:T(8,128)}, f32[5,125,256]{2,1,0:T(8,128)}) custom-call(f32[5,125,256]{2,1,0:T(8,128)} %get-tuple-element.4.resid, f32[40,256]{1,0:T(8,128)} %get-tuple-element.5.second_h, bf16[128,16]{1,0:T(8,128)(2,1)} %constant.20.clone.pro2_h), custom_call_target="tpu_custom_call" | custom-call | tf_op jit(solution)/shard_map/prolongation/pallas_call | solution.py:437

commit v6 on v5

--- a/solution.py
+++ b/solution.py
@@ -108,7 +108,7 @@
     (
         uh, ul, qs,
         ohs, ohm, tr, snd_g, snd_m, snd_n, rcv_g, rcv_m, rcv_n,
-        ohr, ohrm, nlh, nll, resl, ohc, st_hot, blks, mine, resv, mine2, ext, arr_g, arr_m,
+        ohr, ohrm, nlh, nll, resl, ohc, st_hot, blks, mine, resv, mine2, ext01, ext23, ext4, arr_g, arr_m,
         in_sem, st_sem, snd_sem, rcv_sem, out_sem,
     ) = scratch[21:]
     g = lax.axis_index("grp")
@@ -118,6 +118,22 @@
     far = jnp.where(lax.rem(g, 4) == 3, 1, 0)
     prev, nxt = jnp.maximum(g - 1, 0), jnp.minimum(g + 1, n_grp - 1)
 
+    def side(t):
+        return jnp.where(t == 0, prev, nxt), jnp.where(t == 0, has_prev, has_next)
+
+    barrier = pltpu.get_barrier_semaphore()
+    def greet(device):
+        pl.semaphore_signal(barrier, inc=1, device_id=device, device_id_type=MESH)
+
+    for t in (far, 1 - far):
+
+        @pl.when(side(t)[1])
+        def _(t=t):
+            greet((side(t)[0], 0))
+            greet((side(t)[0], 1))
+
+    greet((g, other))
+
     loads = [None] + [pltpu.make_async_copy(sources[i], scratch[i], in_sem.at[i]) for i in range(1, 21)]
     fields = [pltpu.make_async_copy(sources[0].at[v], st.at[v], st_sem.at[v]) for v in range(5)]
     for c in loads[1:7] + fields + loads[7:8]:
@@ -129,22 +145,6 @@
             if i not in seen:
                 seen.add(i)
                 loads[i].wait()
-
-    barrier = pltpu.get_barrier_semaphore()
-    def greet(device):
-        pl.semaphore_signal(barrier, inc=1, device_id=device, device_id_type=MESH)
-
-    greet((g, other))
-
-    @pl.when(has_prev)
-    def _():
-        greet((prev, 0))
-        greet((prev, 1))
-
-    @pl.when(has_next)
-    def _():
-        greet((nxt, 0))
-        greet((nxt, 1))
 
     @pl.when(jnp.logical_not(has_prev))
     def _():
@@ -172,7 +172,9 @@
     snd_n[6:8, :] = jnp.zeros((2, 128), jnp.int32)
 
     for f in range(6):
-        ext[f * 128 : f * 128 + 128, :] = hot(places[f : f + 1, :], 0, 128)
+        ext01[f * 64 : f * 64 + 64, :] = hot(places[f : f + 1, 0:256], 0, 64)
+        ext23[f * 64 : f * 64 + 64, :] = hot(places[f : f + 1, 256:512], 48, 64)
+        ext4[f * 32 : f * 32 + 32, :] = hot(places[f : f + 1, 512:640], 96, 32)
 
     for c in loads[8:]:
         c.start()
@@ -181,10 +183,12 @@
         hi, lo = halves(padded(st[v]))
         uh[v * 128 : v * 128 + 128, :] = hi
         ul[v * 128 : v * 128 + 128, :] = lo
-    for f in range(6):
-        e = ext[f * 128 : f * 128 + 128, :]
-        tr[0:128, f * 256 : f * 256 + 256] = dot(e, uh[...]).astype(BF)
-        tr[128:256, f * 256 : f * 256 + 256] = dot(e, ul[...]).astype(BF)
+    for u, top in ((uh, 0), (ul, 128)):
+        x, y, z = dot(ext01[...], u[0:256, :]), dot(ext23[...], u[256:512, :]), dot(ext4[...], u[512:640, :])
+        for f in range(6):
+            xf, yf, zf = x[f * 64 : f * 64 + 64], y[f * 64 : f * 64 + 64], z[f * 32 : f * 32 + 32]
+            rows = [xf[:48], xf[48:] + yf[:16], yf[16:48], yf[48:] + zf[:16], zf[16:]]
+            tr[top : top + 128, f * 256 : f * 256 + 256] = jnp.concatenate(rows, axis=0).astype(BF)
 
     def remote(src, dst, i, j, device):
         return pltpu.make_async_remote_copy(
@@ -195,9 +199,6 @@
     pl.semaphore_wait(barrier, 1 + 2 * has_prev.astype(jnp.int32) + 2 * has_next.astype(jnp.int32))
     c_nbr = remote(snd_n, rcv_n, 0, 0, (g, other))
     c_nbr.start()
-    def side(t):
-        return jnp.where(t == 0, prev, nxt), jnp.where(t == 0, has_prev, has_next)
-
     c_grp = []
     for t in (far, 1 - far):
         group, there = side(t)
@@ -358,21 +359,22 @@
 
 def last_kernel(resid, second_h, pro2_h, resid_out, corr_out, second, pro2, corr, held, sem):
     loads = [pltpu.make_async_copy(second_h, second, sem.at[0]), pltpu.make_async_copy(pro2_h, pro2, sem.at[1])]
-    loads += [pltpu.make_async_copy(resid.at[v], held.at[v], sem.at[2 + v]) for v in range(5)]
+    whole = pltpu.make_async_copy(resid, held, sem.at[2])
     for c in loads:
         c.start()
+    whole.start()
+    for c in loads:
+        c.wait()
     copies = []
-    loads[0].wait()
-    loads[1].wait()
     for v in range(5):
         corr[v] = dot(pro2[...], stacked(second[v * 8 : v * 8 + 8, :]))[:125]
-        loads[2 + v].wait()
-        c = pltpu.make_async_copy(held.at[v], resid_out.at[v], sem.at[7 + v])
+        c = pltpu.make_async_copy(corr.at[v], corr_out.at[v], sem.at[4 + v])
         c.start()
         copies.append(c)
-        c = pltpu.make_async_copy(corr.at[v], corr_out.at[v], sem.at[12 + v])
-        c.start()
-        copies.append(c)
+    whole.wait()
+    c = pltpu.make_async_copy(held, resid_out, sem.at[3])
+    c.start()
+    copies.append(c)
     for c in copies:
         c.wait()
 
@@ -420,7 +422,9 @@
             pltpu.VMEM((40, 256), F32),
             pltpu.VMEM((5, 125, 256), F32),
             pltpu.VMEM((40, 256), F32),
-            pltpu.VMEM((768, 640), BF),
+            pltpu.VMEM((384, 256), BF),
+            pltpu.VMEM((384, 256), BF),
+            pltpu.VMEM((192, 128), BF),
             pltpu.VMEM((2, 256, 256), BF),
             pltpu.VMEM((256, 128), BF),
             pltpu.SemaphoreType.DMA((21,)),
@@ -444,7 +448,7 @@
             pltpu.VMEM((128, 16), BF),
             pltpu.VMEM((5, 125, 256), F32),
             pltpu.VMEM((5, 125, 256), F32),
-            pltpu.SemaphoreType.DMA((17,)),
+            pltpu.SemaphoreType.DMA((9,)),
         ],
         compiler_params=pltpu.CompilerParams(vmem_limit_bytes=60 * 1024 * 1024),
         name="prolongation",

time: 25.1 us -> 24.7 us (0.984)
  Pallas kernels: 24.3 us -> 23.9 us
    pallas_call x1, Pallas kernels: 2.42 us -> 2.05 us  [shards(): pl.pallas_call(last_kernel, out_shape=(field, field), in_specs=[hbm, hbm,...]
where the time goes in v6:
time: 24.7 us; the launch traced here: 24.6 us
  Pallas kernels  23.9 us (97%)
  between operations  0.64 us (3%)
    pallas_call x1, Pallas kernels, shards(): pl.pallas_call(functools.partial(main_kernel, n_grp), out_shape=(field, j...  21.9 us
    pallas_call x1, Pallas kernels, shards(): pl.pallas_call(last_kernel, out_shape=(field, field), in_specs=[hbm, hbm,...  2.05 us

profile of v6, /device:TPU:257, one launch (start us, length us, event | category | flops | bytes accessed | tf_op | source)
XLA Modules:
  0.0 24.6 jit_solution(9143908864702028076)
XLA Ops:
  0.6 21.9 %residual_and_sweeps.1 = (f32[5,125,256]{2,1,0:T(8,128)}, f32[40,256]{1,0:T(8,128)}) custom-call(f32[5,125,256]{2,1,0:T(8,128)} %refs_0_.1, s32[1,2,128]{2,1,0:T(2,128)} %refs_1_.1, s32[1,2,256]{2,1,0:T(2,128)} %refs_2_.1, s32[1,2]{1,0:T(1,128)} %refs_3_.1, s32[1,2]{1,0:T(1,128)} %refs_4_.1, s32[8,640]{1,0:T(8,128)} %constant.14.clone.refs_5_, ...), custom_call_target="tpu_custom_call" | custom-call | tf_op jit(solution)/shard_map/residual_and_sweeps/pallas_call | solution.py:395
  22.5 2.1 %prolongation.1 = (f32[5,125,256]{2,1,0:T(8,128)}, f32[5,125,256]{2,1,0:T(8,128)}) custom-call(f32[5,125,256]{2,1,0:T(8,128)} %get-tuple-element.4.resid, f32[40,256]{1,0:T(8,128)} %get-tuple-element.5.second_h, bf16[128,16]{1,0:T(8,128)(2,1)} %constant.20.clone.pro2_h), custom_call_target="tpu_custom_call" | custom-call | tf_op jit(solution)/shard_map/prolongation/pallas_call | solution.py:441

commit v7 on v6

--- a/solution.py
+++ b/solution.py
@@ -108,7 +108,7 @@
     (
         uh, ul, qs,
         ohs, ohm, tr, snd_g, snd_m, snd_n, rcv_g, rcv_m, rcv_n,
-        ohr, ohrm, nlh, nll, resl, ohc, st_hot, blks, mine, resv, mine2, ext01, ext23, ext4, arr_g, arr_m,
+        ohr, ohrm, nlh, nll, resl, ohc, st_hot, s_hot, first_weight, blks, mine, resv, mine2, ext01, ext23, ext4, arr_g, arr_m,
         in_sem, st_sem, snd_sem, rcv_sem, out_sem,
     ) = scratch[21:]
     g = lax.axis_index("grp")
@@ -148,13 +148,13 @@
 
     @pl.when(jnp.logical_not(has_prev))
     def _():
-        rcv_g[0] = jnp.zeros((128, 256), F32)
+        rcv_g[0] = jnp.zeros((2, 128, 128), F32)
         blks[0] = jnp.zeros((40, 256), F32)
         blks[1] = jnp.zeros((40, 256), F32)
 
     @pl.when(jnp.logical_not(has_next))
     def _():
-        rcv_g[1] = jnp.zeros((128, 256), F32)
+        rcv_g[1] = jnp.zeros((2, 128, 128), F32)
         blks[4] = jnp.zeros((40, 256), F32)
         blks[5] = jnp.zeros((40, 256), F32)
 
@@ -203,10 +203,12 @@
     for t in (far, 1 - far):
         group, there = side(t)
         picked = dot(tr[...], ohs[t])
-        snd_g[t] = picked[:128] + picked[128:]
-        c = remote(snd_g.at[t], rcv_g.at[1 - t], 1 + t, 2 - t, (group, m))
-        pl.when(there)(c.start)
-        c_grp.append((there, c))
+        whole = picked[:128] + picked[128:]
+        for h in range(2):
+            snd_g[t, h] = whole[:, h * 128 : h * 128 + 128]
+            c = remote(snd_g.at[t, h], rcv_g.at[1 - t, h], (1, 9)[h] + t, (2, 11)[h] - t, (group, m))
+            pl.when(there)(c.start)
+            c_grp.append((there, c))
     picked = dot(tr[...], ohm[...])
     snd_m[...] = picked[:128] + picked[128:]
     c_mem = remote(snd_m, rcv_m, 3, 3, (g, other))
@@ -250,6 +252,10 @@
     ones_before = ones_before.astype(jnp.int32)
     target = jnp.where(owner[...] == 1, 128 + ones_before, lane_g - ones_before)
     st_hot[...] = hot(target, 0, 256)
+    s_hot[...] = st_hot[...].astype(F32).T.astype(BF)
+    cd = cdiag[...]
+    first_weight[...] = (0.8 * 0.064) / cd
+    weight = 0.8 / cd
 
     gfa = g_coarse[...]
     gg = exact(gfa, small[0:8, :]) * small[56:104, :]
@@ -279,15 +285,22 @@
         rest0 = rest0 + (part[:40] + part[40:])
     for t in (1 - far, far):
         group, there = side(t)
-        pl.when(there)(remote(snd_g.at[t], rcv_g.at[t], 1 + t, 1 + t, (group, m)).wait_recv)
-        arr_g[t] = take(rcv_g.at[t])
-        z = dot(by_face[...], arr_g[t])
-        for f in range(6):
-            part = dot(stacked(z[f * 48 : f * 48 + 40]), ohr[t, f])
-            rest0 = rest0 + (part[:40] + part[40:])
-    cd = cdiag[...]
-    first = (0.8 * 0.064) * rest0 / cd
-    packed = lax.dot_general(stacked(first), st_hot[...], (((1,), (1,)), ((), ())), preferred_element_type=F32)
+        halves_of = [remote(snd_g.at[t, h], rcv_g.at[t, h], 1 + t, (1, 10)[h] + t, (group, m)) for h in range(2)]
+        for h in range(2):
+            pl.when(there)(halves_of[h].wait_recv)
+            arr_g[t, :, h * 128 : h * 128 + 128] = take(rcv_g.at[t, h])
+            if t is far:
+                z = dot(by_face[...], arr_g[t, :, h * 128 : h * 128 + 128])
+                for f in range(6):
+                    part = dot(stacked(z[f * 48 : f * 48 + 40]), ohr[t, f, h * 128 : h * 128 + 128, :])
+                    rest0 = rest0 + (part[:40] + part[40:])
+        if t is not far:
+            z = dot(by_face[...], arr_g[t])
+            for f in range(6):
+                part = dot(stacked(z[f * 48 : f * 48 + 40]), ohr[t, f])
+                rest0 = rest0 + (part[:40] + part[40:])
+    first = rest0 * first_weight[...]
+    packed = dot(stacked(first), s_hot[...])
     mine[...] = packed[:40] + packed[40:]
     c_two = []
     for t in (far, 1 - far):
@@ -312,7 +325,6 @@
     c_out = pltpu.make_async_copy(resv, resid_out, out_sem.at[0])
     c_out.start()
     inner = exact(qq, first)
-    weight = 0.8 / cd
     base = 1.2 * first - weight * inner
 
     def arrived(place):
@@ -405,10 +417,10 @@
             pltpu.VMEM((2, 1536, 256), BF),
             pltpu.VMEM((1536, 128), BF),
             pltpu.VMEM((256, 1536), BF),
-            pltpu.VMEM((2, 128, 256), F32),
+            pltpu.VMEM((2, 2, 128, 128), F32),
             pltpu.VMEM((128, 128), F32),
             pltpu.VMEM((8, 128), jnp.int32),
-            pltpu.VMEM((2, 128, 256), F32),
+            pltpu.VMEM((2, 2, 128, 128), F32),
             pltpu.VMEM((128, 128), F32),
             pltpu.VMEM((8, 128), jnp.int32),
             pltpu.VMEM((2, 6, 256, 256), BF),
@@ -418,6 +430,8 @@
             pltpu.VMEM((640, 256), F32),
             pltpu.VMEM((2, 3, 256, 768), BF),
             pltpu.VMEM((256, 256), BF),
+            pltpu.VMEM((256, 256), BF),
+            pltpu.VMEM((40, 256), F32),
             pltpu.VMEM((6, 40, 256), F32),
             pltpu.VMEM((40, 256), F32),
             pltpu.VMEM((5, 125, 256), F32),
@@ -429,8 +443,8 @@
             pltpu.VMEM((256, 128), BF),
             pltpu.SemaphoreType.DMA((21,)),
             pltpu.SemaphoreType.DMA((5,)),
-            pltpu.SemaphoreType.DMA((9,)),
-            pltpu.SemaphoreType.DMA((10,)),
+            pltpu.SemaphoreType.DMA((11,)),
+            pltpu.SemaphoreType.DMA((12,)),
             pltpu.SemaphoreType.DMA((2,)),
         ],
         compiler_params=pltpu.CompilerParams(

time: 24.7 us -> 24.8 us (level)
  no operation moved by 1% of the time
where the time goes in v7:
time: 24.8 us; the launch traced here: 24.6 us
  Pallas kernels  24 us (97%)
  between operations  0.64 us (3%)
    pallas_call x1, Pallas kernels, shards(): pl.pallas_call(functools.partial(main_kernel, n_grp), out_shape=(field, j...  21.9 us
    pallas_call x1, Pallas kernels, shards(): pl.pallas_call(last_kernel, out_shape=(field, field), in_specs=[hbm, hbm,...  2.05 us

profile of v7, /device:TPU:257, one launch (start us, length us, event | category | flops | bytes accessed | tf_op | source)
XLA Modules:
  0.0 24.6 jit_solution(6643953490706922599)
XLA Ops:
  0.6 21.9 %residual_and_sweeps.1 = (f32[5,125,256]{2,1,0:T(8,128)}, f32[40,256]{1,0:T(8,128)}) custom-call(f32[5,125,256]{2,1,0:T(8,128)} %refs_0_.1, s32[1,2,128]{2,1,0:T(2,128)} %refs_1_.1, s32[1,2,256]{2,1,0:T(2,128)} %refs_2_.1, s32[1,2]{1,0:T(1,128)} %refs_3_.1, s32[1,2]{1,0:T(1,128)} %refs_4_.1, s32[8,640]{1,0:T(8,128)} %constant.14.clone.refs_5_, ...), custom_call_target="tpu_custom_call" | custom-call | tf_op jit(solution)/shard_map/residual_and_sweeps/pallas_call | solution.py:407
  22.5 2.1 %prolongation.1 = (f32[5,125,256]{2,1,0:T(8,128)}, f32[5,125,256]{2,1,0:T(8,128)}) custom-call(f32[5,125,256]{2,1,0:T(8,128)} %get-tuple-element.4.resid, f32[40,256]{1,0:T(8,128)} %get-tuple-element.5.second_h, bf16[128,16]{1,0:T(8,128)(2,1)} %constant.20.clone.pro2_h), custom_call_target="tpu_custom_call" | custom-call | tf_op jit(solution)/shard_map/prolongation/pallas_call | solution.py:455

commit v8 on v6

--- a/solution.py
+++ b/solution.py
@@ -115,7 +115,7 @@
     m = lax.axis_index("mem")
     other = 1 - m
     has_prev, has_next = g > 0, g < n_grp - 1
-    far = jnp.where(lax.rem(g, 4) == 3, 1, 0)
+    far = jnp.where(g == 0, 1, jnp.where((lax.rem(g, 4) == 3) & has_next, 1, 0))
     prev, nxt = jnp.maximum(g - 1, 0), jnp.minimum(g + 1, n_grp - 1)
 
     def side(t):
@@ -196,21 +196,22 @@
             device_id=device, device_id_type=MESH,
         )
 
-    pl.semaphore_wait(barrier, 1 + 2 * has_prev.astype(jnp.int32) + 2 * has_next.astype(jnp.int32))
     c_nbr = remote(snd_n, rcv_n, 0, 0, (g, other))
-    c_nbr.start()
     c_grp = []
     for t in (far, 1 - far):
         group, there = side(t)
         picked = dot(tr[...], ohs[t])
         snd_g[t] = picked[:128] + picked[128:]
         c = remote(snd_g.at[t], rcv_g.at[1 - t], 1 + t, 2 - t, (group, m))
+        if t is far:
+            pl.semaphore_wait(barrier, 1 + 2 * has_prev.astype(jnp.int32) + 2 * has_next.astype(jnp.int32))
         pl.when(there)(c.start)
         c_grp.append((there, c))
     picked = dot(tr[...], ohm[...])
     snd_m[...] = picked[:128] + picked[128:]
     c_mem = remote(snd_m, rcv_m, 3, 3, (g, other))
     c_mem.start()
+    c_nbr.start()
 
     base_mem = 1536 + other * 128
 

time: 24.7 us -> 24.2 us (0.980)
  Pallas kernels: 23.9 us -> 23.4 us
    pallas_call x1, Pallas kernels: 21.9 us -> 21.3 us  [shards(): pl.pallas_call(functools.partial(main_kernel, n_grp), out_shape=(field, j...]
where the time goes in v8:
time: 24.2 us; the launch traced here: 24 us
  Pallas kernels  23.4 us (97%)
  between operations  0.64 us (3%)
    pallas_call x1, Pallas kernels, shards(): pl.pallas_call(functools.partial(main_kernel, n_grp), out_shape=(field, j...  21.3 us
    pallas_call x1, Pallas kernels, shards(): pl.pallas_call(last_kernel, out_shape=(field, field), in_specs=[hbm, hbm,...  2.05 us

profile of v8, /device:TPU:257, one launch (start us, length us, event | category | flops | bytes accessed | tf_op | source)
XLA Modules:
  0.0 24.0 jit_solution(5092132549112476073)
XLA Ops:
  0.6 21.3 %residual_and_sweeps.1 = (f32[5,125,256]{2,1,0:T(8,128)}, f32[40,256]{1,0:T(8,128)}) custom-call(f32[5,125,256]{2,1,0:T(8,128)} %refs_0_.1, s32[1,2,128]{2,1,0:T(2,128)} %refs_1_.1, s32[1,2,256]{2,1,0:T(2,128)} %refs_2_.1, s32[1,2]{1,0:T(1,128)} %refs_3_.1, s32[1,2]{1,0:T(1,128)} %refs_4_.1, s32[8,640]{1,0:T(8,128)} %constant.14.clone.refs_5_, ...), custom_call_target="tpu_custom_call" | custom-call | tf_op jit(solution)/shard_map/residual_and_sweeps/pallas_call | solution.py:396
  22.0 2.1 %prolongation.1 = (f32[5,125,256]{2,1,0:T(8,128)}, f32[5,125,256]{2,1,0:T(8,128)}) custom-call(f32[5,125,256]{2,1,0:T(8,128)} %get-tuple-element.4.resid, f32[40,256]{1,0:T(8,128)} %get-tuple-element.5.second_h, bf16[128,16]{1,0:T(8,128)(2,1)} %constant.20.clone.pro2_h), custom_call_target="tpu_custom_call" | custom-call | tf_op jit(solution)/shard_map/prolongation/pallas_call | solution.py:442

commit v9 on v8

--- a/solution.py
+++ b/solution.py
@@ -221,9 +221,10 @@
         at = pl.multiple_of(f * 128, 128)
         nlh[pl.ds(at, 128), :] = acc[:128].astype(BF)
         nll[pl.ds(at, 128), :] = acc[128:].astype(BF)
-        ohr[0, f] = hot(row, 1792, 256)
-        ohr[1, f] = hot(row, 2048, 256)
-        ohrm[f] = hot(row, base_mem, 128)
+        wide = pl.ds(pl.multiple_of(f * 256, 256), 256)
+        ohr[0, wide, :] = hot(row, 1792, 256)
+        ohr[1, wide, :] = hot(row, 2048, 256)
+        ohrm[pl.ds(at, 128), :] = hot(row, base_mem, 128)
         return carry
 
     need(7)
@@ -274,18 +275,18 @@
 
     c_mem.wait_recv()
     arr_m[...] = take(rcv_m)
-    z = dot(by_face[...], arr_m[...])
-    for f in range(6):
-        part = dot(stacked(z[f * 48 : f * 48 + 40]), ohrm[f])
-        rest0 = rest0 + (part[:40] + part[40:])
+
+    def restricted(columns, places):
+        z = dot(by_face[...], columns)
+        part = dot(jnp.concatenate([stacked(z[f * 48 : f * 48 + 40]) for f in range(6)], axis=1), places)
+        return part[:40] + part[40:]
+
+    rest0 = rest0 + restricted(arr_m[...], ohrm[...])
     for t in (1 - far, far):
         group, there = side(t)
         pl.when(there)(remote(snd_g.at[t], rcv_g.at[t], 1 + t, 1 + t, (group, m)).wait_recv)
         arr_g[t] = take(rcv_g.at[t])
-        z = dot(by_face[...], arr_g[t])
-        for f in range(6):
-            part = dot(stacked(z[f * 48 : f * 48 + 40]), ohr[t, f])
-            rest0 = rest0 + (part[:40] + part[40:])
+        rest0 = rest0 + restricted(arr_g[t], ohr[t])
     cd = cdiag[...]
     first = (0.8 * 0.064) * rest0 / cd
     packed = lax.dot_general(stacked(first), st_hot[...], (((1,), (1,)), ((), ())), preferred_element_type=F32)
@@ -302,7 +303,9 @@
     c_own.start()
 
     for f in range(6):
-        acc = dot(arr_g[0], ohr[0, f]) + dot(arr_g[1], ohr[1, f]) + dot(arr_m[...], ohrm[f])
+        wide = slice(f * 256, f * 256 + 256)
+        acc = dot(arr_g[0], ohr[0, wide, :]) + dot(arr_g[1], ohr[1, wide, :])
+        acc = acc + dot(arr_m[...], ohrm[f * 128 : f * 128 + 128, :])
         nlh[f * 128 : f * 128 + 128, :] += acc[:128].astype(BF)
         nll[f * 128 : f * 128 + 128, :] += acc[128:].astype(BF)
     need(20)
@@ -412,8 +415,8 @@
             pltpu.VMEM((2, 128, 256), F32),
             pltpu.VMEM((128, 128), F32),
             pltpu.VMEM((8, 128), jnp.int32),
-            pltpu.VMEM((2, 6, 256, 256), BF),
-            pltpu.VMEM((6, 128, 256), BF),
+            pltpu.VMEM((2, 1536, 256), BF),
+            pltpu.VMEM((768, 256), BF),
             pltpu.VMEM((768, 256), BF),
             pltpu.VMEM((768, 256), BF),
             pltpu.VMEM((640, 256), F32),

time: 24.2 us -> 24.2 us (level)
  no operation moved by 1% of the time
where the time goes in v9:
time: 24.2 us; the launch traced here: 24.1 us
  Pallas kernels  23.4 us (97%)
  between operations  0.64 us (3%)
    pallas_call x1, Pallas kernels, shards(): pl.pallas_call(functools.partial(main_kernel, n_grp), out_shape=(field, j...  21.4 us
    pallas_call x1, Pallas kernels, shards(): pl.pallas_call(last_kernel, out_shape=(field, field), in_specs=[hbm, hbm,...  2.05 us

profile of v9, /device:TPU:257, one launch (start us, length us, event | category | flops | bytes accessed | tf_op | source)
XLA Modules:
  0.0 24.1 jit_solution(13453564489473059465)
XLA Ops:
  0.6 21.4 %residual_and_sweeps.1 = (f32[5,125,256]{2,1,0:T(8,128)}, f32[40,256]{1,0:T(8,128)}) custom-call(f32[5,125,256]{2,1,0:T(8,128)} %refs_0_.1, s32[1,2,128]{2,1,0:T(2,128)} %refs_1_.1, s32[1,2,256]{2,1,0:T(2,128)} %refs_2_.1, s32[1,2]{1,0:T(1,128)} %refs_3_.1, s32[1,2]{1,0:T(1,128)} %refs_4_.1, s32[8,640]{1,0:T(8,128)} %constant.14.clone.refs_5_, ...), custom_call_target="tpu_custom_call" | custom-call | tf_op jit(solution)/shard_map/residual_and_sweeps/pallas_call | solution.py:399
  22.0 2.1 %prolongation.1 = (f32[5,125,256]{2,1,0:T(8,128)}, f32[5,125,256]{2,1,0:T(8,128)}) custom-call(f32[5,125,256]{2,1,0:T(8,128)} %get-tuple-element.4.resid, f32[40,256]{1,0:T(8,128)} %get-tuple-element.5.second_h, bf16[128,16]{1,0:T(8,128)(2,1)} %constant.20.clone.pro2_h), custom_call_target="tpu_custom_call" | custom-call | tf_op jit(solution)/shard_map/prolongation/pallas_call | solution.py:445
